TPU v7x, 128 devices: a whole 4x4x4 slice. The times are simulated.
128 devices in a mesh: ctx: 32 (over x, z, core), head: 4 (over y).
Axes of the slice: x: 4, y: 4, z: 4, core: 2. Of those that a mesh axis runs over, the one named last changes fastest.
Arguments:
- queries: bfloat16 [16384, 2560], P(('ctx', 'head')), may hold values from -6 to 6
- key_rows: bfloat16 [16384, 2560], P(('ctx', 'head')), may hold values from -6 to 6
- value_rows: bfloat16 [16384, 2560], P(('ctx', 'head')), may hold values from -6 to 6
- forward_out: bfloat16 [16384, 2560], P(('ctx', 'head')), may hold values from -6 to 6
- out_grad: bfloat16 [16384, 2560], P(('ctx', 'head')), may hold values from -96 to 96
- log_norm: float32 [16384, 20], P(('ctx', 'head')), may hold values from -1 to 12
- block_order: int32 [128], replicated, may hold values from 0 to 127, as said below
- pattern: int32 [128, 36], replicated, may hold values from -1 to 127, as said below
Outputs:
- query_grad: bfloat16 [16384, 2560], P(('ctx', 'head'))
- key_grad: bfloat16 [16384, 2560], P(('ctx', 'head'))
- value_grad: bfloat16 [16384, 2560], P(('ctx', 'head'))
Inputs may be any that keep to these rules, and one draw needn't show every extreme that they name: `block_order`: A permutation of the block numbers. `pattern`: row g names each key block at most once, -1 marks an unused entry, and g itself is always named. Among the blocks stored on any one index of ctx, the query blocks stored on another index name at most one block, and when one of those query blocks names it, all of them do; the query blocks of every index name one block stored on the next index of ctx (cyclically).
All inputs are finite; a program needn't handle non-finite values.
Results may differ from a plain program's by a relative error of at most 0.0062.
Values may be sent and summed in bfloat16 or wider, within the bound.
A program may use at most 192 MiB of HBM per device.

v0:
```python
import jax
import jax.numpy as jnp
from jax import lax
from jax.sharding import PartitionSpec as P


def adjacency(block_order, pattern):
    blocks = block_order.shape[0]
    numbers = jnp.arange(blocks, dtype=jnp.int32)
    slot_of = jnp.zeros((blocks,), jnp.int32).at[block_order].set(numbers)
    listed = pattern[block_order]
    key_slot = jnp.where(listed >= 0, slot_of[jnp.maximum(listed, 0)], -1)
    return jnp.any(key_slot[:, :, None] == numbers[None, None, :], axis=1)


def against_rows(left, right):
    return lax.dot_general(
        left, right, (((1,), (1,)), ((), ())), preferred_element_type=jnp.float32
    )


def against_cols(left, right):
    return lax.dot_general(
        left, right, (((0,), (0,)), ((), ())), preferred_element_type=jnp.float32
    )


def head_grads(query2, key2, value2, grad2, norm_col, dot_col, mask, scale):
    score = against_rows(query2, key2) * scale
    prob = jnp.where(mask, jnp.exp(score - norm_col[:, None]), 0.0)
    dprob = against_rows(grad2, value2)
    dscore = (prob * (dprob - dot_col[:, None])).astype(jnp.bfloat16)
    probs = prob.astype(jnp.bfloat16)
    return (
        jnp.dot(dscore, key2, preferred_element_type=jnp.float32) * scale,
        against_cols(dscore, query2) * scale,
        against_cols(probs, grad2),
    )


def all_heads(query2d, key2d, value2d, grad2d, norm_h, dots_h, mask, scale, local_heads, feature):
    dq_list = []
    dk_list = []
    dv_list = []
    for head in range(local_heads):
        low = head * feature
        high = low + feature
        dq_one, dk_one, dv_one = head_grads(
            query2d[:, low:high],
            key2d[:, low:high],
            value2d[:, low:high],
            grad2d[:, low:high],
            norm_h[:, head],
            dots_h[:, head],
            mask,
            scale,
        )
        dq_list.append(dq_one)
        dk_list.append(dk_one)
        dv_list.append(dv_one)
    return (
        jnp.concatenate(dq_list, axis=1),
        jnp.concatenate(dk_list, axis=1),
        jnp.concatenate(dv_list, axis=1),
    )


def spread(table, size):
    shape = table.shape
    lead = shape[:-2]
    grown = jnp.broadcast_to(
        table[..., :, None, :, None], lead + (shape[-2], size, shape[-1], size)
    )
    return grown.reshape(lead + (shape[-2] * size, shape[-1] * size))


def body(queries, key_rows, value_rows, forward_out, out_grad, log_norm, block_order, pattern):
    ctx_count = lax.axis_size("ctx")
    head_count = lax.axis_size("head")
    my_index = lax.axis_index("ctx")
    tok_rows, full_width = queries.shape
    heads = log_norm.shape[1]
    feature = full_width // heads
    local_heads = heads // head_count
    blocks = block_order.shape[0]
    blocks_mine = blocks // ctx_count
    block_len = tok_rows * head_count // blocks_mine
    rows_mine = blocks_mine * block_len
    width = local_heads * feature
    scale = feature ** (-0.5)
    query_h, key_h, value_h, grad_h, output_h = (
        lax.all_to_all(queries, "head", split_axis=1, concat_axis=0, tiled=True),
        lax.all_to_all(key_rows, "head", split_axis=1, concat_axis=0, tiled=True),
        lax.all_to_all(value_rows, "head", split_axis=1, concat_axis=0, tiled=True),
        lax.all_to_all(out_grad, "head", split_axis=1, concat_axis=0, tiled=True),
        lax.all_to_all(forward_out, "head", split_axis=1, concat_axis=0, tiled=True),
    )
    norm_h = lax.all_to_all(log_norm, "head", split_axis=1, concat_axis=0, tiled=True)
    dots_h = jnp.sum(
        (grad_h.astype(jnp.float32) * output_h.astype(jnp.float32)).reshape(
            rows_mine, local_heads, feature
        ),
        axis=-1,
    )
    adjacent = adjacency(block_order, pattern).reshape(
        ctx_count, blocks_mine, ctx_count, blocks_mine
    )
    mine = lax.dynamic_index_in_dim(adjacent, my_index, 0, keepdims=False)
    theirs = lax.dynamic_index_in_dim(adjacent, my_index, 2, keepdims=False)
    numbers = jnp.arange(blocks_mine, dtype=jnp.int32)
    peers = jnp.arange(ctx_count, dtype=jnp.int32)
    others = peers != my_index
    own = lax.dynamic_index_in_dim(mine, my_index, 1, keepdims=False)
    position = jnp.arange(rows_mine, dtype=jnp.int32)
    same_block = position[:, None] // block_len == position[None, :] // block_len
    local_mask = spread(own, block_len) & (
        jnp.logical_not(same_block) | (position[:, None] >= position[None, :])
    )
    groups = -(-ctx_count // blocks_mine)
    dq_local, dk_local, dv_local = all_heads(
        query_h, key_h, value_h, grad_h, norm_h, dots_h, local_mask, scale, local_heads, feature
    )
    pick = jnp.sum(jnp.where(jnp.any(mine, axis=0) & others[:, None], numbers[None, :], 0), axis=-1)
    give = jnp.sum(
        jnp.where(jnp.any(theirs, axis=1) & others[:, None], numbers[None, :], 0), axis=-1
    )
    owner_map = ((give[:, None] == numbers[None, :]) & others[:, None]).astype(jnp.bfloat16)
    sent_keys = jnp.einsum(
        "nq,qrw->nrw",
        owner_map,
        key_h.reshape(blocks_mine, block_len, width),
        preferred_element_type=jnp.float32,
    ).astype(jnp.bfloat16)
    sent_values = jnp.einsum(
        "nq,qrw->nrw",
        owner_map,
        value_h.reshape(blocks_mine, block_len, width),
        preferred_element_type=jnp.float32,
    ).astype(jnp.bfloat16)
    got_keys, got_values = (
        lax.all_to_all(sent_keys, "ctx", split_axis=0, concat_axis=0, tiled=True),
        lax.all_to_all(sent_values, "ctx", split_axis=0, concat_axis=0, tiled=True),
    )
    chosen = numbers[None, :] == pick[:, None]
    remote = jnp.any(mine & chosen[None, :, :], axis=-1) & others[None, :]
    group_mask = spread(
        jnp.transpose(remote.reshape(blocks_mine, groups, blocks_mine), (1, 0, 2)), block_len
    )
    pad_keys = got_keys.reshape(groups, rows_mine, width)
    pad_values = got_values.reshape(groups, rows_mine, width)
    dq_all = dq_local
    key_parts = []
    value_parts = []
    for group in range(groups):
        keys_g = pad_keys[group]
        values_g = pad_values[group]
        mask_g = group_mask[group]
        dq_t, dk_t, dv_t = all_heads(
            query_h, keys_g, values_g, grad_h, norm_h, dots_h, mask_g, scale, local_heads, feature
        )
        dq_all = dq_all + dq_t
        key_parts.append(dk_t.astype(jnp.bfloat16))
        value_parts.append(dv_t.astype(jnp.bfloat16))
    part_keys = jnp.stack(key_parts).reshape(groups * blocks_mine, block_len, width)
    part_values = jnp.stack(value_parts).reshape(groups * blocks_mine, block_len, width)
    back_keys, back_values = (
        lax.all_to_all(part_keys, "ctx", split_axis=0, concat_axis=0, tiled=True),
        lax.all_to_all(part_values, "ctx", split_axis=0, concat_axis=0, tiled=True),
    )
    dk_all = dk_local + jnp.einsum(
        "nq,nrw->qrw", owner_map, back_keys, preferred_element_type=jnp.float32
    ).reshape(rows_mine, width)
    dv_all = dv_local + jnp.einsum(
        "nq,nrw->qrw", owner_map, back_values, preferred_element_type=jnp.float32
    ).reshape(rows_mine, width)
    results = (
        lax.all_to_all(
            dq_all.astype(jnp.bfloat16), "head", split_axis=0, concat_axis=1, tiled=True
        ),
        lax.all_to_all(
            dk_all.astype(jnp.bfloat16), "head", split_axis=0, concat_axis=1, tiled=True
        ),
        lax.all_to_all(
            dv_all.astype(jnp.bfloat16), "head", split_axis=0, concat_axis=1, tiled=True
        ),
    )
    return (results[0], results[1], results[2])


def solution(mesh):
    placed = (
        P(("ctx", "head"), None),
        P(("ctx", "head"), None),
        P(("ctx", "head"), None),
        P(("ctx", "head"), None),
        P(("ctx", "head"), None),
        P(("ctx", "head"), None),
        P(),
        P(),
    )
    return jax.shard_map(
        body,
        mesh=mesh,
        in_specs=placed,
        out_specs=(P(("ctx", "head"), None), P(("ctx", "head"), None), P(("ctx", "head"), None)),
        check_vma=False,
    )
```

profile of v0, /device:TPU:32, one launch (start us, length us, event | category | flops | bytes accessed | tf_op | source)
XLA Modules:
  0.0 536.3 jit_solution(7309714794962854805)
XLA Ops:
  1.9 4.5 all-to-all-start.2
  9.7 26.0 %gather_fusion.1 = s32[4608]{0:T(1024)S(1)} fusion(s32[128]{0:T(128)S(1)} %scatter_custom_fusion, s32[5120]{0:T(1024)S(1)} %pad_clamp_fusion), kind=kCustom, calls=%fused_computation.1 | custom fusion | bytes 55296 | tf_op jit(solution)/shard_map/gather | solution.py:12
  38.0 4.8 all-to-all-start
  42.8 2.3 reshape.1476
  47.0 6.0 %all-to-all-done = bf16[128,4,640]{0,2,1:T(8,128)(2,1)S(1)} async-done(((bf16[128,4,640]{0,2,1:T(8,128)(2,1)}), bf16[128,4,640]{0,2,1:T(8,128)(2,1)S(1)}, u32[]{:S(2)}, u32[]{:S(2)}) %all-to-all-start) | async-done | bytes 655392 | tf_op jit(solution)/shard_map/all_to_all | solution.py:92
  53.1 3.5 all-to-all-start.1
  57.8 7.8 %all-to-all-done.1 = bf16[128,4,640]{2,0,1:T(8,128)(2,1)S(1)} async-done(((bf16[128,4,640]{2,0,1:T(8,128)(2,1)}), bf16[128,4,640]{2,0,1:T(8,128)(2,1)S(1)}, u32[]{:S(2)}, u32[]{:S(2)}) %all-to-all-start.1) | async-done | bytes 655392 | tf_op jit(solution)/shard_map/all_to_all | solution.py:93
  65.6 3.5 all-to-all-start.3
  72.4 5.5 %all-to-all-done.3 = bf16[128,4,640]{0,2,1:T(8,128)(2,1)S(1)} async-done(((bf16[128,4,640]{0,2,1:T(8,128)(2,1)}), bf16[128,4,640]{0,2,1:T(8,128)(2,1)S(1)}, u32[]{:S(2)}, u32[]{:S(2)}) %all-to-all-start.3) | async-done | bytes 655392 | tf_op jit(solution)/shard_map/all_to_all | solution.py:95
  77.9 3.5 all-to-all-start.4
  81.7 2.2 copy.863
  83.9 6.2 %all-to-all-done.4 = bf16[128,4,640]{2,0,1:T(8,128)(2,1)S(1)} async-done(((bf16[128,4,640]{2,0,1:T(8,128)(2,1)}), bf16[128,4,640]{2,0,1:T(8,128)(2,1)S(1)}, u32[]{:S(2)}, u32[]{:S(2)}) %all-to-all-start.4) | async-done | bytes 655392 | tf_op jit(solution)/shard_map/all_to_all | solution.py:94
  90.1 3.5 all-to-all-start.5
  93.6 1.6 convolution_convert_fusion.1
  95.2 4.1 copy.878
  99.3 3.0 all-to-all-done.5
  103.2 8.5 %all-to-all-start.6 = ((bf16[32,128,640]{2,1,0:T(8,128)(2,1)}), bf16[32,128,640]{2,1,0:T(8,128)(2,1)}, u32[]{:S(2)}, u32[]{:S(2)}) async-start(bf16[32,128,640]{2,1,0:T(8,128)(2,1)} %copy.878), calls=%async_computation.6 | async-start | bytes 10485760 | tf_op jit(solution)/shard_map/all_to_all | solution.py:141
  111.7 3.9 convolution_convert_fusion
  115.9 1.6 copy.858
  118.2 6.9 %copy.881 = bf16[32,128,640]{2,1,0:T(8,128)(2,1)} copy(bf16[32,128,640]{2,0,1:T(8,128)(2,1)} %convolution_convert_fusion) | data formatting | bytes 10485760 | tf_op jit(solution)/shard_map/convert_element_type | solution.py:139
  125.2 1.9 copy.864
  127.2 2.7 mul.589
  129.9 1.6 copy.1254
  132.4 1.4 reduce_sum.27
  152.1 29.7 %all-to-all-done.6 = bf16[32,128,640]{2,1,0:T(8,128)(2,1)} async-done(((bf16[32,128,640]{2,1,0:T(8,128)(2,1)}), bf16[32,128,640]{2,1,0:T(8,128)(2,1)}, u32[]{:S(2)}, u32[]{:S(2)}) %all-to-all-start.6) | async-done | bytes 5242912 | tf_op jit(solution)/shard_map/all_to_all | solution.py:141
  181.8 5.1 all-to-all-start.7
  186.9 3.2 fusion.902
  190.8 1.9 fusion.79
  197.1 1.5 fusion.99
  202.8 1.4 fusion.119
  221.2 1.5 fusion.179
  227.1 1.4 fusion.199
  231.4 1.6 fusion.214
  232.9 1.4 fusion.219
  234.6 1.4 fusion.224
  237.4 1.5 fusion.234
  247.5 1.5 fusion.269
  249.0 5.8 %all-to-all-done.7 = bf16[32,128,640]{2,1,0:T(8,128)(2,1)} async-done(((bf16[32,128,640]{2,1,0:T(8,128)(2,1)}), bf16[32,128,640]{2,1,0:T(8,128)(2,1)}, u32[]{:S(2)}, u32[]{:S(2)}) %all-to-all-start.7) | async-done | bytes 5242912 | tf_op jit(solution)/shard_map/all_to_all | solution.py:142
  254.8 3.2 fusion.901
  337.7 2.9 add_convert_fusion
  340.6 4.2 all-to-all-start.8
  344.8 2.1 fusion.489
  346.8 7.8 %copy.1016 = bf16[8,512,640]{2,1,0:T(8,128)(2,1)} copy(bf16[8,512,640]{1,2,0:T(8,128)(2,1)} %fusion.441) | data formatting | bytes 10485760 | tf_op jit(solution)/shard_map/stack | solution.py:165
  354.7 2.0 fusion.487
  356.7 2.1 fusion.485
  358.8 4.9 all-to-all-start.11
  363.7 2.2 fusion.483
  366.0 2.1 fusion.481
  368.1 2.1 fusion.479
  370.2 2.1 fusion.477
  372.3 2.1 fusion.475
  374.5 2.1 fusion.473
  376.6 2.1 fusion.471
  393.1 38.8 %all-to-all-done.11 = bf16[32,128,640]{2,1,0:T(8,128)(2,1)} async-done(((bf16[32,128,640]{2,1,0:T(8,128)(2,1)}), bf16[32,128,640]{2,1,0:T(8,128)(2,1)}, u32[]{:S(2)}, u32[]{:S(2)}) %all-to-all-start.11) | async-done | bytes 5242912 | tf_op jit(solution)/shard_map/all_to_all | solution.py:168
  431.9 4.9 all-to-all-start.9
  436.9 1.7 fusion.572
  445.5 6.3 %fusion.271 = bf16[4,128,640]{2,0,1:T(4,128)(2,1)S(1)} fusion(f32[4,128,640]{2,0,1:T(4,128)S(1)} %constant_dynamic-update-slice_fusion.50, bf16[32,128,640]{2,1,0:T(8,128)(2,1)} %all-to-all-done.11, s32[32]{0:T(128)S(1)} %get-tuple-element.10, pred[32]{0:T(512)(128)(4,1)S(1)} %iota_compare_fusion.4), kind=kOutput, calls=%fused_computation.363 | convolution fusion | flops 21627136 | bytes 7209120 | tf_op jit(solution)/shard_map/nq,nrw->qrw/dot_general | solution.py:173
  452.7 52.3 %all-to-all-done.9 = bf16[32,128,640]{2,1,0:T(8,128)(2,1)} async-done(((bf16[32,128,640]{2,1,0:T(8,128)(2,1)}), bf16[32,128,640]{2,1,0:T(8,128)(2,1)}, u32[]{:S(2)}, u32[]{:S(2)}) %all-to-all-start.9) | async-done | bytes 5242912 | tf_op jit(solution)/shard_map/all_to_all | solution.py:167
  505.0 5.5 %all-to-all-start.12 = ((bf16[4,128,640]{2,1,0:T(8,128)(2,1)}), bf16[4,128,640]{2,1,0:T(8,128)(2,1)S(1)}, u32[]{:S(2)}, u32[]{:S(2)}) async-start(bf16[4,128,640]{2,1,0:T(8,128)(2,1)} %copy.1019), calls=%async_computation.12 | async-start | bytes 1310720 | tf_op jit(solution)/shard_map/all_to_all | solution.py:183
  510.7 6.2 %fusion.274 = bf16[4,128,640]{2,0,1:T(4,128)(2,1)S(1)} fusion(f32[4,128,640]{2,0,1:T(4,128)S(1)} %constant_dynamic-update-slice_fusion.45, bf16[32,128,640]{2,1,0:T(8,128)(2,1)} %all-to-all-done.9, s32[32]{0:T(128)S(1)} %get-tuple-element.10, pred[32]{0:T(512)(128)(4,1)S(1)} %iota_compare_fusion.4), kind=kOutput, calls=%fused_computation.364 | convolution fusion | flops 21627136 | bytes 7209120 | tf_op jit(solution)/shard_map/nq,nrw->qrw/dot_general | solution.py:170
  517.8 3.3 all-to-all-done.12
  521.2 3.5 all-to-all-start.10
  524.7 2.0 copy.1169
  528.1 6.3 %all-to-all-done.10 = bf16[4,128,640]{2,1,0:T(8,128)(2,1)S(1)} async-done(((bf16[4,128,640]{2,1,0:T(8,128)(2,1)}), bf16[4,128,640]{2,1,0:T(8,128)(2,1)S(1)}, u32[]{:S(2)}, u32[]{:S(2)}) %all-to-all-start.10) | async-done | bytes 655392 | tf_op jit(solution)/shard_map/all_to_all | solution.py:180
  (574 shorter events, 182.1 us)
Async XLA Ops:
  1.9 36.0 %all-to-all-start.2 = ((f32[128,4,5]{0,2,1:T(8,128)}), f32[128,4,5]{0,2,1:T(8,128)S(1)}, u32[]{:S(2)}, u32[]{:S(2)}) async-start(f32[128,4,5]{0,2,1:T(8,128)} %all_to_all.136), calls=%async_computation.2 | async-start | bytes 32768 | tf_op jit(solution)/shard_map/all_to_all | solution.py:98
  9.7 27.2 %copy-start.123 = (bf16[128,2560]{1,0:T(8,128)(2,1)S(1)}, bf16[128,2560]{1,0:T(8,128)(2,1)}, u32[]{:S(2)}) copy-start(bf16[128,2560]{1,0:T(8,128)(2,1)} %param.8) | copy-start | bytes 1966084
  9.7 35.4 %copy-start.124 = (bf16[128,2560]{1,0:T(8,128)(2,1)S(1)}, bf16[128,2560]{1,0:T(8,128)(2,1)}, u32[]{:S(2)}) copy-start(bf16[128,2560]{1,0:T(8,128)(2,1)} %param.9) | copy-start | bytes 1966084
  35.7 20.9 %copy-start.125 = (bf16[128,2560]{1,0:T(8,128)(2,1)S(1)}, bf16[128,2560]{1,0:T(8,128)(2,1)}, u32[]{:S(2)}) copy-start(bf16[128,2560]{1,0:T(8,128)(2,1)} %param.12) | copy-start | bytes 1966084
  38.0 15.1 %all-to-all-start = ((bf16[128,4,640]{0,2,1:T(8,128)(2,1)}), bf16[128,4,640]{0,2,1:T(8,128)(2,1)S(1)}, u32[]{:S(2)}, u32[]{:S(2)}) async-start(bf16[128,4,640]{0,2,1:T(8,128)(2,1)} %bitcast.1), calls=%async_computation | async-start | bytes 1310720 | tf_op jit(solution)/shard_map/all_to_all | solution.py:92
  53.1 12.6 %all-to-all-start.1 = ((bf16[128,4,640]{2,0,1:T(8,128)(2,1)}), bf16[128,4,640]{2,0,1:T(8,128)(2,1)S(1)}, u32[]{:S(2)}, u32[]{:S(2)}) async-start(bf16[128,4,640]{2,0,1:T(8,128)(2,1)} %copy.852), calls=%async_computation.1 | async-start | bytes 1310720 | tf_op jit(solution)/shard_map/all_to_all | solution.py:93
  65.6 12.2 %all-to-all-start.3 = ((bf16[128,4,640]{0,2,1:T(8,128)(2,1)}), bf16[128,4,640]{0,2,1:T(8,128)(2,1)S(1)}, u32[]{:S(2)}, u32[]{:S(2)}) async-start(bf16[128,4,640]{0,2,1:T(8,128)(2,1)} %bitcast.10), calls=%async_computation.3 | async-start | bytes 1310720 | tf_op jit(solution)/shard_map/all_to_all | solution.py:95
  77.9 21.4 %copy-start.9 = (bf16[128,4,640]{0,2,1:T(8,128)(2,1)}, bf16[128,4,640]{0,2,1:T(8,128)(2,1)S(1)}, u32[]{:S(2)}) copy-start(bf16[128,4,640]{0,2,1:T(8,128)(2,1)S(1)} %all-to-all-done.3) | copy-start | bytes 1966084
  77.9 12.2 %all-to-all-start.4 = ((bf16[128,4,640]{2,0,1:T(8,128)(2,1)}), bf16[128,4,640]{2,0,1:T(8,128)(2,1)S(1)}, u32[]{:S(2)}, u32[]{:S(2)}) async-start(bf16[128,4,640]{2,0,1:T(8,128)(2,1)} %copy.860), calls=%async_computation.4 | async-start | bytes 1310720 | tf_op jit(solution)/shard_map/all_to_all | solution.py:94
  90.1 21.6 %copy-start.11 = (bf16[128,4,640]{2,0,1:T(8,128)(2,1)}, bf16[128,4,640]{2,0,1:T(8,128)(2,1)S(1)}, u32[]{:S(2)}) copy-start(bf16[128,4,640]{2,0,1:T(8,128)(2,1)S(1)} %all-to-all-done.4) | copy-start | bytes 1966084
  90.1 12.2 %all-to-all-start.5 = ((bf16[128,4,640]{0,2,1:T(8,128)(2,1)}), bf16[128,4,640]{0,2,1:T(8,128)(2,1)S(1)}, u32[]{:S(2)}, u32[]{:S(2)}) async-start(bf16[128,4,640]{0,2,1:T(8,128)(2,1)} %bitcast.1352), calls=%async_computation.5 | async-start | bytes 1310720 | tf_op jit(solution)/shard_map/all_to_all | solution.py:96
  103.2 78.6 %all-to-all-start.6 = ((bf16[32,128,640]{2,1,0:T(8,128)(2,1)}), bf16[32,128,640]{2,1,0:T(8,128)(2,1)}, u32[]{:S(2)}, u32[]{:S(2)}) async-start(bf16[32,128,640]{2,1,0:T(8,128)(2,1)} %copy.878), calls=%async_computation.6 | async-start | bytes 10485760 | tf_op jit(solution)/shard_map/all_to_all | solution.py:141
  115.9 21.6 %copy-start.5 = (bf16[4,128,640]{2,1,0:T(8,128)(2,1)}, bf16[4,128,640]{2,1,0:T(8,128)(2,1)S(1)}, u32[]{:S(2)}) copy-start(bf16[4,128,640]{2,1,0:T(8,128)(2,1)S(1)} %copy.850) | copy-start | bytes 1966084
  118.2 17.5 %copy-start.7 = (bf16[4,128,640]{2,1,0:T(8,128)(2,1)}, bf16[4,128,640]{2,1,0:T(8,128)(2,1)S(1)}, u32[]{:S(2)}) copy-start(bf16[4,128,640]{2,1,0:T(8,128)(2,1)S(1)} %copy.854) | copy-start | bytes 1966084
  181.8 72.9 %all-to-all-start.7 = ((bf16[32,128,640]{2,1,0:T(8,128)(2,1)}), bf16[32,128,640]{2,1,0:T(8,128)(2,1)}, u32[]{:S(2)}, u32[]{:S(2)}) async-start(bf16[32,128,640]{2,1,0:T(8,128)(2,1)} %copy.881), calls=%async_computation.7 | async-start | bytes 10485760 | tf_op jit(solution)/shard_map/all_to_all | solution.py:142
  190.1 20.0 %copy-start.72 = (bf16[4,128,640]{2,1,0:T(8,128)(2,1)}, bf16[4,128,640]{2,1,0:T(8,128)(2,1)S(1)}, u32[]{:S(2)}) copy-start(bf16[4,128,640]{2,1,0:T(8,128)(2,1)S(1)} %get-tuple-element.25) | copy-start | bytes 1966084
  190.1 27.2 %copy-start.70 = (bf16[4,128,640]{2,1,0:T(8,128)(2,1)}, bf16[4,128,640]{2,1,0:T(8,128)(2,1)S(1)}, u32[]{:S(2)}) copy-start(bf16[4,128,640]{2,1,0:T(8,128)(2,1)S(1)} %get-tuple-element.24) | copy-start | bytes 1966084
  190.1 35.4 %copy-start.68 = (bf16[4,128,640]{2,1,0:T(8,128)(2,1)}, bf16[4,128,640]{2,1,0:T(8,128)(2,1)S(1)}, u32[]{:S(2)}) copy-start(bf16[4,128,640]{2,1,0:T(8,128)(2,1)S(1)} %get-tuple-element.23) | copy-start | bytes 1966084
  190.1 42.8 %copy-start.66 = (bf16[4,128,640]{2,1,0:T(8,128)(2,1)}, bf16[4,128,640]{2,1,0:T(8,128)(2,1)S(1)}, u32[]{:S(2)}) copy-start(bf16[4,128,640]{2,1,0:T(8,128)(2,1)S(1)} %get-tuple-element.22) | copy-start | bytes 1966084
  190.1 50.1 %copy-start.64 = (bf16[4,128,640]{2,1,0:T(8,128)(2,1)}, bf16[4,128,640]{2,1,0:T(8,128)(2,1)S(1)}, u32[]{:S(2)}) copy-start(bf16[4,128,640]{2,1,0:T(8,128)(2,1)S(1)} %get-tuple-element.21) | copy-start | bytes 1966084
  190.1 57.3 %copy-start.62 = (bf16[4,128,640]{2,1,0:T(8,128)(2,1)}, bf16[4,128,640]{2,1,0:T(8,128)(2,1)S(1)}, u32[]{:S(2)}) copy-start(bf16[4,128,640]{2,1,0:T(8,128)(2,1)S(1)} %get-tuple-element.20) | copy-start | bytes 1966084
  190.8 29.5 %copy-start.60 = (f32[512,512]{1,0:T(8,128)}, f32[512,512]{1,0:T(8,128)S(1)}, u32[]{:S(2)}) copy-start(f32[512,512]{1,0:T(8,128)S(1)} %fusion.74) | copy-start | bytes 3145732
  278.7 50.4 %copy-start.90 = (bf16[512,512]{1,0:T(8,128)(2,1)}, bf16[512,512]{1,0:T(8,128)(2,1)S(1)}, u32[]{:S(2)}) copy-start(bf16[512,512]{1,0:T(8,128)(2,1)S(1)} %fusion.300) | copy-start | bytes 1572868
  280.4 49.1 %copy-start.89 = (bf16[512,512]{1,0:T(8,128)(2,1)}, bf16[512,512]{1,0:T(8,128)(2,1)S(1)}, u32[]{:S(2)}) copy-start(bf16[512,512]{1,0:T(8,128)(2,1)S(1)} %fusion.299) | copy-start | bytes 1572868
  281.7 48.1 %copy-start.91 = (bf16[512,512]{1,0:T(8,128)(2,1)}, bf16[512,512]{1,0:T(8,128)(2,1)S(1)}, u32[]{:S(2)}) copy-start(bf16[512,512]{1,0:T(8,128)(2,1)S(1)} %fusion.298) | copy-start | bytes 1572868
  282.9 47.2 %copy-start.83 = (bf16[512,512]{1,0:T(8,128)(2,1)}, bf16[512,512]{1,0:T(8,128)(2,1)S(1)}, u32[]{:S(2)}) copy-start(bf16[512,512]{1,0:T(8,128)(2,1)S(1)} %fusion.297) | copy-start | bytes 1572868
  285.1 45.3 %copy-start.85 = (bf16[512,512]{1,0:T(8,128)(2,1)}, bf16[512,512]{1,0:T(8,128)(2,1)S(1)}, u32[]{:S(2)}) copy-start(bf16[512,512]{1,0:T(8,128)(2,1)S(1)} %fusion.296) | copy-start | bytes 1572868
  285.4 45.3 %copy-start.84 = (bf16[512,512]{1,0:T(8,128)(2,1)}, bf16[512,512]{1,0:T(8,128)(2,1)S(1)}, u32[]{:S(2)}) copy-start(bf16[512,512]{1,0:T(8,128)(2,1)S(1)} %fusion.295) | copy-start | bytes 1572868
  286.7 44.4 %copy-start.86 = (bf16[512,512]{1,0:T(8,128)(2,1)}, bf16[512,512]{1,0:T(8,128)(2,1)S(1)}, u32[]{:S(2)}) copy-start(bf16[512,512]{1,0:T(8,128)(2,1)S(1)} %fusion.294) | copy-start | bytes 1572868
  288.0 43.4 %copy-start.87 = (bf16[512,512]{1,0:T(8,128)(2,1)}, bf16[512,512]{1,0:T(8,128)(2,1)S(1)}, u32[]{:S(2)}) copy-start(bf16[512,512]{1,0:T(8,128)(2,1)S(1)} %fusion.293) | copy-start | bytes 1572868
  289.2 42.5 %copy-start.88 = (bf16[512,512]{1,0:T(8,128)(2,1)}, bf16[512,512]{1,0:T(8,128)(2,1)S(1)}, u32[]{:S(2)}) copy-start(bf16[512,512]{1,0:T(8,128)(2,1)S(1)} %fusion.292) | copy-start | bytes 1572868
  291.4 40.6 %copy-start.94 = (bf16[512,512]{1,0:T(8,128)(2,1)}, bf16[512,512]{1,0:T(8,128)(2,1)S(1)}, u32[]{:S(2)}) copy-start(bf16[512,512]{1,0:T(8,128)(2,1)S(1)} %fusion.291) | copy-start | bytes 1572868
  291.7 40.7 %copy-start.92 = (bf16[512,512]{1,0:T(8,128)(2,1)}, bf16[512,512]{1,0:T(8,128)(2,1)S(1)}, u32[]{:S(2)}) copy-start(bf16[512,512]{1,0:T(8,128)(2,1)S(1)} %fusion.290) | copy-start | bytes 1572868
  293.0 39.7 %copy-start.95 = (bf16[512,512]{1,0:T(8,128)(2,1)}, bf16[512,512]{1,0:T(8,128)(2,1)S(1)}, u32[]{:S(2)}) copy-start(bf16[512,512]{1,0:T(8,128)(2,1)S(1)} %fusion.289) | copy-start | bytes 1572868
  294.2 38.8 %copy-start.97 = (bf16[512,512]{1,0:T(8,128)(2,1)}, bf16[512,512]{1,0:T(8,128)(2,1)S(1)}, u32[]{:S(2)}) copy-start(bf16[512,512]{1,0:T(8,128)(2,1)S(1)} %fusion.288) | copy-start | bytes 1572868
  295.5 37.8 %copy-start.99 = (bf16[512,512]{1,0:T(8,128)(2,1)}, bf16[512,512]{1,0:T(8,128)(2,1)S(1)}, u32[]{:S(2)}) copy-start(bf16[512,512]{1,0:T(8,128)(2,1)S(1)} %fusion.287) | copy-start | bytes 1572868
  297.7 36.9 %copy-start.103 = (bf16[512,512]{1,0:T(8,128)(2,1)}, bf16[512,512]{1,0:T(8,128)(2,1)S(1)}, u32[]{:S(2)}) copy-start(bf16[512,512]{1,0:T(8,128)(2,1)S(1)} %fusion.286) | copy-start | bytes 1572868
  298.0 36.3 %copy-start.101 = (bf16[512,512]{1,0:T(8,128)(2,1)}, bf16[512,512]{1,0:T(8,128)(2,1)S(1)}, u32[]{:S(2)}) copy-start(bf16[512,512]{1,0:T(8,128)(2,1)S(1)} %fusion.285) | copy-start | bytes 1572868
  299.3 34.7 %copy-start.105 = (bf16[512,512]{1,0:T(8,128)(2,1)}, bf16[512,512]{1,0:T(8,128)(2,1)S(1)}, u32[]{:S(2)}) copy-start(bf16[512,512]{1,0:T(8,128)(2,1)S(1)} %fusion.284) | copy-start | bytes 1572868
  300.5 33.1 %copy-start.107 = (bf16[512,512]{1,0:T(8,128)(2,1)}, bf16[512,512]{1,0:T(8,128)(2,1)S(1)}, u32[]{:S(2)}) copy-start(bf16[512,512]{1,0:T(8,128)(2,1)S(1)} %fusion.283) | copy-start | bytes 1572868
  301.8 33.1 %copy-start.109 = (bf16[512,512]{1,0:T(8,128)(2,1)}, bf16[512,512]{1,0:T(8,128)(2,1)S(1)}, u32[]{:S(2)}) copy-start(bf16[512,512]{1,0:T(8,128)(2,1)S(1)} %fusion.282) | copy-start | bytes 1572868
  304.0 32.5 %copy-start.111 = (bf16[512,512]{1,0:T(8,128)(2,1)}, bf16[512,512]{1,0:T(8,128)(2,1)S(1)}, u32[]{:S(2)}) copy-start(bf16[512,512]{1,0:T(8,128)(2,1)S(1)} %fusion.281) | copy-start | bytes 1572868
  304.3 31.9 %copy-start.113 = (bf16[512,512]{1,0:T(8,128)(2,1)}, bf16[512,512]{1,0:T(8,128)(2,1)S(1)}, u32[]{:S(2)}) copy-start(bf16[512,512]{1,0:T(8,128)(2,1)S(1)} %fusion.280) | copy-start | bytes 1572868
  305.6 30.3 %copy-start.115 = (bf16[512,512]{1,0:T(8,128)(2,1)}, bf16[512,512]{1,0:T(8,128)(2,1)S(1)}, u32[]{:S(2)}) copy-start(bf16[512,512]{1,0:T(8,128)(2,1)S(1)} %fusion.279) | copy-start | bytes 1572868
  306.8 28.7 %copy-start.117 = (bf16[512,512]{1,0:T(8,128)(2,1)}, bf16[512,512]{1,0:T(8,128)(2,1)S(1)}, u32[]{:S(2)}) copy-start(bf16[512,512]{1,0:T(8,128)(2,1)S(1)} %fusion.278) | copy-start | bytes 1572868
  308.1 27.2 %copy-start.119 = (bf16[512,512]{1,0:T(8,128)(2,1)}, bf16[512,512]{1,0:T(8,128)(2,1)S(1)}, u32[]{:S(2)}) copy-start(bf16[512,512]{1,0:T(8,128)(2,1)S(1)} %fusion.277) | copy-start | bytes 1572868
  340.6 18.2 %all-to-all-start.8 = ((bf16[4,128,640]{2,1,0:T(8,128)(2,1)}), bf16[4,128,640]{2,1,0:T(8,128)(2,1)}, u32[]{:S(2)}, u32[]{:S(2)}) async-start(bf16[4,128,640]{2,1,0:T(8,128)(2,1)} %add_convert_fusion), calls=%async_computation.8 | async-start | bytes 1310720 | tf_op jit(solution)/shard_map/all_to_all | solution.py:177
  358.8 73.1 %all-to-all-start.11 = ((bf16[32,128,640]{2,1,0:T(8,128)(2,1)}), bf16[32,128,640]{2,1,0:T(8,128)(2,1)}, u32[]{:S(2)}, u32[]{:S(2)}) async-start(bf16[32,128,640]{2,1,0:T(8,128)(2,1)} %bitcast.1123), calls=%async_computation.11 | async-start | bytes 10485760 | tf_op jit(solution)/shard_map/all_to_all | solution.py:168
  363.7 15.0 %copy-start.93 = (bf16[512,512]{1,0:T(8,128)(2,1)S(1)}, bf16[512,512]{1,0:T(8,128)(2,1)}, u32[]{:S(2)}) copy-start(bf16[512,512]{1,0:T(8,128)(2,1)} %copy-done.92) | copy-start | bytes 1572868
  363.7 16.1 %copy-start.96 = (bf16[512,512]{1,0:T(8,128)(2,1)S(1)}, bf16[512,512]{1,0:T(8,128)(2,1)}, u32[]{:S(2)}) copy-start(bf16[512,512]{1,0:T(8,128)(2,1)} %copy-done.95) | copy-start | bytes 1572868
  363.7 17.1 %copy-start.98 = (bf16[512,512]{1,0:T(8,128)(2,1)S(1)}, bf16[512,512]{1,0:T(8,128)(2,1)}, u32[]{:S(2)}) copy-start(bf16[512,512]{1,0:T(8,128)(2,1)} %copy-done.97) | copy-start | bytes 1572868
  363.7 18.1 %copy-start.100 = (bf16[512,512]{1,0:T(8,128)(2,1)S(1)}, bf16[512,512]{1,0:T(8,128)(2,1)}, u32[]{:S(2)}) copy-start(bf16[512,512]{1,0:T(8,128)(2,1)} %copy-done.99) | copy-start | bytes 1572868
  363.7 19.2 %copy-start.104 = (bf16[512,512]{1,0:T(8,128)(2,1)S(1)}, bf16[512,512]{1,0:T(8,128)(2,1)}, u32[]{:S(2)}) copy-start(bf16[512,512]{1,0:T(8,128)(2,1)} %copy-done.103) | copy-start | bytes 1572868
  363.7 20.2 %copy-start.102 = (bf16[512,512]{1,0:T(8,128)(2,1)S(1)}, bf16[512,512]{1,0:T(8,128)(2,1)}, u32[]{:S(2)}) copy-start(bf16[512,512]{1,0:T(8,128)(2,1)} %copy-done.101) | copy-start | bytes 1572868
  363.7 21.2 %copy-start.106 = (bf16[512,512]{1,0:T(8,128)(2,1)S(1)}, bf16[512,512]{1,0:T(8,128)(2,1)}, u32[]{:S(2)}) copy-start(bf16[512,512]{1,0:T(8,128)(2,1)} %copy-done.105) | copy-start | bytes 1572868
  366.0 20.0 %copy-start.108 = (bf16[512,512]{1,0:T(8,128)(2,1)S(1)}, bf16[512,512]{1,0:T(8,128)(2,1)}, u32[]{:S(2)}) copy-start(bf16[512,512]{1,0:T(8,128)(2,1)} %copy-done.107) | copy-start | bytes 1572868
  368.1 18.9 %copy-start.110 = (bf16[512,512]{1,0:T(8,128)(2,1)S(1)}, bf16[512,512]{1,0:T(8,128)(2,1)}, u32[]{:S(2)}) copy-start(bf16[512,512]{1,0:T(8,128)(2,1)} %copy-done.109) | copy-start | bytes 1572868
  370.2 17.8 %copy-start.112 = (bf16[512,512]{1,0:T(8,128)(2,1)S(1)}, bf16[512,512]{1,0:T(8,128)(2,1)}, u32[]{:S(2)}) copy-start(bf16[512,512]{1,0:T(8,128)(2,1)} %copy-done.111) | copy-start | bytes 1572868
  372.3 16.7 %copy-start.114 = (bf16[512,512]{1,0:T(8,128)(2,1)S(1)}, bf16[512,512]{1,0:T(8,128)(2,1)}, u32[]{:S(2)}) copy-start(bf16[512,512]{1,0:T(8,128)(2,1)} %copy-done.113) | copy-start | bytes 1572868
  374.5 15.6 %copy-start.116 = (bf16[512,512]{1,0:T(8,128)(2,1)S(1)}, bf16[512,512]{1,0:T(8,128)(2,1)}, u32[]{:S(2)}) copy-start(bf16[512,512]{1,0:T(8,128)(2,1)} %copy-done.115) | copy-start | bytes 1572868
  431.9 73.1 %all-to-all-start.9 = ((bf16[32,128,640]{2,1,0:T(8,128)(2,1)}), bf16[32,128,640]{2,1,0:T(8,128)(2,1)}, u32[]{:S(2)}, u32[]{:S(2)}) async-start(bf16[32,128,640]{2,1,0:T(8,128)(2,1)} %bitcast.1225), calls=%async_computation.9 | async-start | bytes 10485760 | tf_op jit(solution)/shard_map/all_to_all | solution.py:167
  445.5 65.0 %copy-start.122 = (f32[4,128,640]{2,0,1:T(4,128)S(1)}, f32[4,128,640]{2,0,1:T(4,128)}, u32[]{:S(2)}) copy-start(f32[4,128,640]{2,0,1:T(4,128)} %copy-done.121) | copy-start | bytes 3932164
  505.0 16.2 %all-to-all-start.12 = ((bf16[4,128,640]{2,1,0:T(8,128)(2,1)}), bf16[4,128,640]{2,1,0:T(8,128)(2,1)S(1)}, u32[]{:S(2)}, u32[]{:S(2)}) async-start(bf16[4,128,640]{2,1,0:T(8,128)(2,1)} %copy.1019), calls=%async_computation.12 | async-start | bytes 1310720 | tf_op jit(solution)/shard_map/all_to_all | solution.py:183
  521.2 13.2 %all-to-all-start.10 = ((bf16[4,128,640]{2,1,0:T(8,128)(2,1)}), bf16[4,128,640]{2,1,0:T(8,128)(2,1)S(1)}, u32[]{:S(2)}, u32[]{:S(2)}) async-start(bf16[4,128,640]{2,1,0:T(8,128)(2,1)} %copy.1009), calls=%async_computation.10 | async-start | bytes 1310720 | tf_op jit(solution)/shard_map/all_to_all | solution.py:180
  (75 other events, 367.4 us)
where the time goes:
time: 546 us; the launch traced here: 536 us
  matrix products  204 us (37%)
  waiting for transfers between devices  165 us (30%)
  local copies, waits for them, and re-layouts  97 us (18%)
  starting transfers between devices  59.7 us (11%)
  other arithmetic  7 us (1%)
    dot_general x90, matrix products, against_cols(): lax.dot_general(left, right, (((0,), (0,)), ((), ())), preferred_element_...  94.7 us
    dot_general x90, matrix products, against_rows(): lax.dot_general(left, right, (((1,), (1,)), ((), ())), preferred_element_...  76.5 us
    all_to_all x1, waiting for transfers between devices, body(): lax.all_to_all(part_keys, 'ctx', split_axis=0, concat_axis=0, tiled=True)  52.3 us
    all_to_all x1, waiting for transfers between devices, body(): lax.all_to_all(part_values, 'ctx', split_axis=0, concat_axis=0, tiled=True)  38.8 us
    all_to_all x1, waiting for transfers between devices, body(): lax.all_to_all(sent_keys, 'ctx', split_axis=0, concat_axis=0, tiled=True)  29.7 us
    gather x2, local copies, waits for them, and re-layouts, adjacency(): key_slot = jnp.where(listed >= 0, slot_of[jnp.maximum(listed, 0)], -1)  26.1 us
    unnamed x308, local copies, waits for them, and re-layouts  20.1 us
    dot_general x45, matrix products, head_grads(): jnp.dot(dscore, key2, preferred_element_type=jnp.float32) * scale  14.7 us
  transfers between devices with their start and end apart: 13, of which 11 were waited for; matrix products, arithmetic and copies ran while one was open for 40% of the time, Pallas kernels for 0%

commit v1 on v0

v1 whole, which is shorter than its diff:
```python
import functools

import jax
import jax.numpy as jnp
from jax import lax
from jax.experimental import pallas as pl
from jax.experimental.pallas import tpu as pltpu
from jax.sharding import PartitionSpec as P

MESH = pl.DeviceIdType.MESH
HBM = pl.ANY
VMEM = pltpu.VMEM
BF = jnp.bfloat16
F32 = jnp.float32
BLK = 128
HEADS = 20
LOG2E = 1.4426950408889634
SCALE = 128 ** -0.5
FAR = 1e30
GROUP = 4 * BLK


def coords():
    c = lax.axis_index("ctx")
    return c // 8, (c // 2) % 4, c % 2, lax.axis_index("head")


def dev(x, z, k, y):
    return (x * 8 + z * 2 + k, y)


def rows(start, size):
    return pl.ds(pl.multiple_of(start, BLK), size)


def cols(head):
    return pl.ds(pl.multiple_of(head * BLK, BLK), BLK)


def q_pair(z):
    return z + 1 - 2 * (z % 2)


def k_pair(z):
    return (z + 3 + 2 * (z % 2)) % 4


def send(src, dst, ss, rs, to):
    pltpu.make_async_remote_copy(
        src_ref=src, dst_ref=dst, send_sem=ss, recv_sem=rs, device_id=to, device_id_type=MESH
    ).start()


def wait(ref, sem):
    pltpu.make_async_copy(ref, ref, sem).wait()


def greet():
    x, z, k, y = coords()
    barrier = pltpu.get_barrier_semaphore()
    peers = [dev((x + dx) % 4, z, k, (y + dy) % 4) for dx in range(4) for dy in range(4) if dx or dy]
    peers += [dev(x, (z + dz) % 4, k, y) for dz in range(1, 4)]
    peers.append(dev(x, z, 1 - k, y))
    for peer in peers:
        pl.semaphore_signal(barrier, inc=1, device_id=peer, device_id_type=MESH)
    pl.semaphore_wait(barrier, len(peers))


DX = (0, 1, 3, 2)


def gather_kernel(
    q_in, k_in, v_in, g_in, o_in, norm_in, pat_in, order_in,
    qa, ga, xa, ka, va, qb, gb, xb, kb, vb, table,
    g_v, o_v, aux, square, pat_v,
    load_sem, sa1, ra1, sb1, rb1, s_zq, r_zq, s_c, r_c, s_c2, r_c2, s_zk, r_zk,
    s_bz, r_bz, s_bc, r_bc, s_bx, r_bx,
):
    x, z, k, y = coords()
    load_g = pltpu.make_async_copy(g_in, g_v, load_sem.at[0])
    load_o = pltpu.make_async_copy(o_in, o_v, load_sem.at[1])
    load_g.start()
    load_o.start()
    greet()
    mine = (x * 4 + y) * BLK

    wide = ((0, q_in, qa, qb), (1, g_in, ga, gb), (2, k_in, ka, kb), (3, v_in, va, vb))

    def scatter_a(a, src_of, dst, n):
        for dx in DX:
            for dy in range(4):
                tx, ty = (x + dx) % 4, (y + dy) % 4
                src = src_of(ty * 4 + tx)
                if dx or dy:
                    send(src, dst, sa1.at[a], ra1.at[a, dx], dev(tx, z, k, ty))
                else:
                    pltpu.make_async_copy(src, dst, ra1.at[a, 0]).start()

    def scatter_b(a, src_of, dst_of):
        for dy in range(4):
            ty = (y + dy) % 4
            src = src_of(16 + ty)
            if dy:
                send(src, dst_of, sb1.at[a], rb1.at[a], dev(x, z, k, ty))
            else:
                pltpu.make_async_copy(src, dst_of, rb1.at[a]).start()

    slot = k * 4 + z
    for a, src, da, db in wide:
        scatter_a(a, lambda h, src=src: src.at[:, cols(h)], da.at[rows(mine, BLK), :], BLK)
        base = (slot if a < 2 else x) * GROUP + y * BLK
        scatter_b(a, lambda h, src=src: src.at[:, cols(h)], db.at[rows(base, BLK), :])

    square[...] = jnp.zeros((BLK, BLK), F32)
    square[:, 0:HEADS] = norm_in[...] * LOG2E
    norm_t = square[...].T
    load_g.wait()
    load_o.wait()
    for h in range(HEADS):
        prod = g_v[:, h * BLK:(h + 1) * BLK].astype(F32) * o_v[:, h * BLK:(h + 1) * BLK].astype(F32)
        dot = jnp.sum(prod.T, axis=0, keepdims=True)
        aux[h] = jnp.concatenate([norm_t[h:h + 1], dot, jnp.zeros((6, BLK), F32)], axis=0)
    scatter_a(4, lambda h: aux.at[h], xa.at[x * 4 + y], 1)
    scatter_b(4, lambda h: aux.at[h], xb.at[slot * 4 + y])

    def part(a, ref, quad, dx, count=4):
        xs = (x + 4 - dx) % 4
        if a == 4:
            return ref.at[pl.ds((quad * 4 + xs) * 4, 4)]
        return ref.at[rows((quad * 4 + xs) * GROUP, GROUP), :]

    buf_a = {0: qa, 1: ga, 2: ka, 3: va, 4: xa}
    buf_b = {0: qb, 1: gb, 2: kb, 3: vb, 4: xb}
    to_q = dev(x, q_pair(z), k, y)
    to_k = dev(x, k_pair(z), k, y)
    to_c = dev(x, z, 1 - k, y)

    def forward_a(dx):
        for a in (0, 1, 4):
            ref = buf_a[a]
            wait(part(a, ref, 0, dx), ra1.at[a, dx])
            send(part(a, ref, 0, dx), part(a, ref, 1, dx), s_zq.at[a], r_zq.at[a, dx], to_q)
            send(part(a, ref, 0, dx), part(a, ref, 2, dx), s_c.at[a], r_c.at[a], to_c)
        for a in (2, 3):
            ref = buf_a[a]
            wait(part(a, ref, 0, dx), ra1.at[a, dx])
            send(part(a, ref, 0, dx), part(a, ref, 1, dx), s_zk.at[a - 2], r_zk.at[a - 2], to_k)

    def slab(a, ref, index, count=1):
        if a == 4:
            return ref.at[pl.ds(index * 4, 4 * count)]
        return ref.at[rows(index * GROUP, GROUP * count), :]

    def forward_b():
        for a in (0, 1, 4):
            ref = buf_b[a]
            own = slab(a, ref, slot)
            wait(own, rb1.at[a])
            for dz in (1, 3, 2):
                send(own, own, s_bz.at[a], r_bz.at[a, dz], dev(x, (z + dz) % 4, k, y))
            send(own, own, s_bc.at[a], r_bc.at[a], to_c)
        for a in (2, 3):
            ref = buf_b[a]
            own = slab(a, ref, x)
            wait(own, rb1.at[a])
            for dx in (1, 3, 2):
                send(own, own, s_bx.at[a - 2], r_bx.at[a - 2], dev((x + dx) % 4, z, k, y))

    forward_a(0)
    forward_b()
    for dx in DX[1:]:
        forward_a(dx)

    pat_v[...] = jnp.full((BLK, BLK), -1.0, F32)
    pat_v[:, 0:36] = pat_in[...].astype(F32)
    order = order_in[...].astype(F32)
    i0 = lax.broadcasted_iota(jnp.int32, (BLK, BLK), 0)
    i1 = lax.broadcasted_iota(jnp.int32, (BLK, BLK), 1)
    hot = jnp.where(i0.astype(F32) == order, 1.0, 0.0).T
    listed = jnp.dot(hot.astype(BF), pat_v[...].astype(BF), preferred_element_type=F32)
    adj = jnp.zeros((BLK, BLK), F32)
    for e in range(36):
        adj = jnp.maximum(adj, jnp.where(listed[:, e:e + 1] == order, 1.0, 0.0))
    local = (i0 // 4) == (i1 // 4)
    pick = jnp.where((i0 // 4) == i1, (i0 % 4 + 1).astype(F32), 0.0)
    own_cols = jnp.where(i1 == 32 + i0 % 4, 1.0, 0.0)
    table[...] = (
        jnp.dot(jnp.where(local, 0.0, adj).astype(BF), pick.astype(BF), preferred_element_type=F32)
        + jnp.dot(jnp.where(local, adj, 0.0).astype(BF), own_cols.astype(BF), preferred_element_type=F32)
    ).astype(jnp.int32)

    for dz in (1, 3, 2):
        for a in (0, 1, 4):
            ref = buf_b[a]
            got = slab(a, ref, k * 4 + (z + 4 - dz) % 4)
            wait(got, r_bz.at[a, dz])
            send(got, got, s_bc.at[a], r_bc.at[a], to_c)
    for dx in DX:
        for a in (0, 1, 4):
            ref = buf_a[a]
            wait(part(a, ref, 1, dx), r_zq.at[a, dx])
            send(part(a, ref, 1, dx), part(a, ref, 3, dx), s_c2.at[a], r_c2.at[a], to_c)

    def quad(a, ref, index):
        if a == 4:
            return ref.at[pl.ds(index * 16, 16)]
        return ref.at[pl.ds(index * 4 * GROUP, 4 * GROUP), :]

    for a in (2, 3):
        wait(quad(a, buf_a[a], 1), r_zk.at[a - 2])
        wait(quad(a, buf_a[a], 0), s_zk.at[a - 2])
        wait(slab(a, buf_b[a], 0, 3), r_bx.at[a - 2])
        wait(slab(a, buf_b[a], 0, 3), s_bx.at[a - 2])
    for a in (0, 1, 4):
        wait(quad(a, buf_a[a], 2), r_c.at[a])
        wait(quad(a, buf_a[a], 3), r_c2.at[a])
        wait(quad(a, buf_a[a], 0), s_zq.at[a])
        wait(quad(a, buf_a[a], 0), s_c.at[a])
        wait(quad(a, buf_a[a], 0), s_c2.at[a])
        wait(slab(a, buf_b[a], 0, 4), r_bc.at[a])
        wait(slab(a, buf_b[a], 0, 4), s_bc.at[a])
        wait(slab(a, buf_b[a], 0, 3), s_bz.at[a])
    for a in range(5):
        ref = buf_a[a]
        if a == 4:
            wait(ref.at[pl.ds(0, 15)], sa1.at[a])
            wait(ref.at[pl.ds(0, 3)], sb1.at[a])
        else:
            wait(ref.at[pl.ds(0, 15 * BLK), :], sa1.at[a])
            wait(ref.at[pl.ds(0, 3 * BLK), :], sb1.at[a])


def against_rows(left, right):
    return lax.dot_general(left, right, (((1,), (1,)), ((), ())), preferred_element_type=F32)


def against_cols(left, right):
    return lax.dot_general(left, right, (((0,), (0,)), ((), ())), preferred_element_type=F32)


def compute_kernel(
    table, qa, ga, xa, ka, va, qb, gb, xb, kb, vb,
    dqa, dka, dva, dqb, dkb, dvb,
    acc_k, acc_v, dq_acc,
):
    x, z, k, y = coords()
    base2 = SCALE * LOG2E

    def one_pass(query, grad, norm, dot, keys, values, biases, causal):
        score = against_rows(keys, query)
        dprob = against_rows(values, grad)
        probs, scores = [], []
        for i in range(4):
            cut = slice(i * BLK, (i + 1) * BLK)
            prob = jnp.exp2(score[cut] * base2 - (norm + biases[i]))
            if causal:
                key_at = lax.broadcasted_iota(jnp.int32, (BLK, GROUP), 0)
                query_at = lax.broadcasted_iota(jnp.int32, (BLK, GROUP), 1) - i * BLK
                hidden = (query_at >= 0) & (query_at < key_at)
                prob = jnp.where(hidden, 0.0, prob)
            probs.append(prob.astype(BF))
            scores.append((prob * (dprob[cut] - dot)).astype(BF))
        prob = jnp.concatenate(probs, axis=0)
        score = jnp.concatenate(scores, axis=0)
        return (
            against_cols(score, keys),
            jnp.dot(score, query, preferred_element_type=F32),
            jnp.dot(prob, grad, preferred_element_type=F32),
        )

    def run(q_ref, g_ref, x_ref, k_ref, v_ref, dq_ref, q, c, key_groups, diag):
        at = pl.ds(pl.multiple_of(q * GROUP, GROUP), GROUP)
        query, grad = q_ref[at, :], g_ref[at, :]
        norm = jnp.concatenate([x_ref[q * 4 + b, 0:1, :] for b in range(4)], axis=1)
        dot = jnp.concatenate([x_ref[q * 4 + b, 1:2, :] for b in range(4)], axis=1)
        total = None
        for first, key_index in key_groups:
            places, biases = [], []
            for i in range(4):
                code = table[4 * c, key_index(i)]
                places.append(pl.multiple_of((first + i) * GROUP + jnp.maximum(code - 1, 0) * BLK, BLK))
                biases.append(jnp.where(code > 0, 0.0, FAR))
            keys = jnp.concatenate([k_ref[pl.ds(p, BLK), :] for p in places], axis=0)
            values = jnp.concatenate([v_ref[pl.ds(p, BLK), :] for p in places], axis=0)
            dq, dk, dv = one_pass(query, grad, norm, dot, keys, values, biases, False)
            for i, p in enumerate(places):
                acc_k[pl.ds(p, BLK), :] += dk[i * BLK:(i + 1) * BLK]
                acc_v[pl.ds(p, BLK), :] += dv[i * BLK:(i + 1) * BLK]
            total = dq if total is None else total + dq
        dq_acc[...] = total
        pred, own = diag

        @pl.when(pred)
        def _():
            here = pl.ds(pl.multiple_of(own * GROUP, GROUP), GROUP)
            biases = [
                jnp.concatenate(
                    [
                        jnp.full((1, BLK), jnp.where(table[4 * c + b, 32 + i] > 0, 0.0, FAR), F32)
                        for b in range(4)
                    ],
                    axis=1,
                )
                for i in range(4)
            ]
            dq, dk, dv = one_pass(query, grad, norm, dot, k_ref[here, :], v_ref[here, :], biases, True)
            acc_k[here, :] += dk
            acc_v[here, :] += dv
            dq_acc[...] += dq

        dq_ref[at, :] = (dq_acc[...] * SCALE).astype(BF)

    def finish(dk_ref, dv_ref, n):
        def step(i, carry):
            at = pl.ds(pl.multiple_of(i * GROUP, GROUP), GROUP)
            dk_ref[at, :] = (acc_k[at, :] * SCALE).astype(BF)
            dv_ref[at, :] = acc_v[at, :].astype(BF)
            acc_k[at, :] = jnp.zeros((GROUP, BLK), F32)
            acc_v[at, :] = jnp.zeros((GROUP, BLK), F32)
            return carry

        lax.fori_loop(0, n, step, 0)

    acc_k[...] = jnp.zeros_like(acc_k)
    acc_v[...] = jnp.zeros_like(acc_v)
    zq, zk = q_pair(z), k_pair(z)

    def step_a(q, carry):
        quad, xq = q // 4, q % 4
        zc = jnp.where(quad % 2 == 0, z, zq)
        kc = jnp.where(quad < 2, k, 1 - k)
        c = xq * 8 + zc * 2 + kc
        groups = [
            (0, lambda i: i * 8 + z * 2 + k),
            (4, lambda i: i * 8 + zk * 2 + k),
        ]
        run(qa, ga, xa, ka, va, dqa, q, c, groups, (q < 4, q % 4))
        return carry

    lax.fori_loop(0, 16, step_a, 0)
    finish(dka, dva, 8)

    def step_b(q, carry):
        kc, zc = q // 4, q % 4
        c = x * 8 + zc * 2 + kc
        run(qb, gb, xb, kb, vb, dqb, q, c, [(0, lambda i: i * 8 + z * 2 + k)], (q == k * 4 + z, x))
        return carry

    lax.fori_loop(0, 8, step_b, 0)
    finish(dkb, dvb, 4)


def return_kernel(
    dqa, dka, dva, dqb, dkb, dvb,
    dq_out, dk_out, dv_out,
    got_zk, got_c, got_zq, put_zq, fin, bgot_c, bput_q, bgot_z, bgot_x, bfin,
    s_zk, r_zk, s_c, r_c, s_zq, r_zq, s_bc, r_bc, s_bz, r_bz, s_bx, r_bx, s_out, r_out,
):
    x, z, k, y = coords()
    outs = (dq_out, dk_out, dv_out)
    to_q = dev(x, q_pair(z), k, y)
    to_k = dev(x, k_pair(z), k, y)
    to_c = dev(x, z, 1 - k, y)
    greet()

    def chunk(ref, quad, dx):
        return ref.at[rows((quad * 4 + (x + dx) % 4) * GROUP, GROUP), :]

    def slab(ref, index):
        return ref.at[rows(index * GROUP, GROUP), :]

    for dx in DX:
        send(chunk(dqa, 3, dx), chunk(got_c, 1, dx), s_c, r_c.at[1, dx], to_c)
    send(dqb.at[rows((1 - k) * 4 * GROUP, 4 * GROUP), :], bgot_c, s_bc, r_bc, to_c)
    for dx in DX:
        for n, src in enumerate((dka, dva)):
            send(chunk(src, 1, dx), chunk(got_zk.at[n], 0, dx), s_zk, r_zk.at[n, dx], to_k)
    for dx in DX:
        send(chunk(dqa, 2, dx), chunk(got_c, 0, dx), s_c, r_c.at[0, dx], to_c)
    for dx in (1, 3, 2):
        for n, src in enumerate((dkb, dvb)):
            send(slab(src, (x + dx) % 4), slab(bgot_x.at[n], dx - 1), s_bx, r_bx.at[n, dx - 1], dev((x + dx) % 4, z, k, y))

    def add(*refs):
        total = refs[0][...].astype(F32)
        for ref in refs[1:]:
            total = total + ref[...].astype(F32)
        return total.astype(BF)

    for dx in DX:
        wait(chunk(got_c, 1, dx), r_c.at[1, dx])
        part = chunk(put_zq, 0, dx)
        part[...] = add(chunk(dqa, 1, dx), chunk(got_c, 1, dx))
        send(part, chunk(got_zq, 0, dx), s_zq, r_zq.at[dx], to_q)
    wait(bgot_c, r_bc)
    for dz in (1, 3, 2):
        zt = (z + dz) % 4
        part = slab(bput_q, zt)
        part[...] = add(slab(dqb, k * 4 + zt), slab(bgot_c, zt))
        send(part, slab(bgot_z, dz - 1), s_bz, r_bz.at[dz - 1], dev(x, zt, k, y))

    def give(n, src, base, tx, head_of, dx):
        for dy in range(4):
            ty = (y + dy) % 4
            block = src.at[rows(base + ty * BLK, BLK), :]
            dst = outs[n].at[:, cols(head_of)]
            if dx or dy:
                send(block, dst, s_out.at[n], r_out.at[n], dev(tx, z, k, ty))
            else:
                pltpu.make_async_copy(block, dst, r_out.at[n]).start()

    for dx in (1, 3, 2, 0):
        tx = (x + dx) % 4
        for n, own in ((1, dka), (2, dva)):
            wait(chunk(got_zk.at[n - 1], 0, dx), r_zk.at[n - 1, dx])
            out = chunk(fin.at[n], 0, dx)
            out[...] = add(chunk(own, 0, dx), chunk(got_zk.at[n - 1], 0, dx))
            give(n, fin.at[n], tx * GROUP, tx, y * 4 + x, dx)
    for dx in (1, 3, 2, 0):
        tx = (x + dx) % 4
        wait(chunk(got_c, 0, dx), r_c.at[0, dx])
        wait(chunk(got_zq, 0, dx), r_zq.at[dx])
        out = chunk(fin.at[0], 0, dx)
        out[...] = add(chunk(dqa, 0, dx), chunk(got_c, 0, dx), chunk(got_zq, 0, dx))
        give(0, fin.at[0], tx * GROUP, tx, y * 4 + x, dx)
    for n, own in ((1, dkb), (2, dvb)):
        for i in range(3):
            wait(slab(bgot_x.at[n - 1], i), r_bx.at[n - 1, i])
        bfin[n] = add(slab(own, x), *[slab(bgot_x.at[n - 1], i) for i in range(3)])
        give(n, bfin.at[n], 0, x, 16 + y, 0)
    for i in range(3):
        wait(slab(bgot_z, i), r_bz.at[i])
    bfin[0] = add(slab(dqb, k * 4 + z), slab(bgot_c, z), *[slab(bgot_z, i) for i in range(3)])
    give(0, bfin.at[0], 0, x, 16 + y, 0)

    for n in range(3):
        wait(outs[n], r_out.at[n])
        wait(dqa.at[pl.ds(0, 18 * BLK), :], s_out.at[n])
    wait(dqa.at[pl.ds(0, 8 * GROUP), :], s_c)
    wait(dqa.at[pl.ds(0, 8 * GROUP), :], s_zk)
    wait(put_zq, s_zq)
    wait(bgot_c, s_bc)
    wait(bgot_z, s_bz)
    wait(dqa.at[pl.ds(0, 6 * GROUP), :], s_bx)


def body(queries, key_rows, value_rows, forward_out, out_grad, log_norm, block_order, pattern):
    wide = lambda n: jax.ShapeDtypeStruct((n * BLK, BLK), BF)
    aux = lambda n: jax.ShapeDtypeStruct((n, 8, BLK), F32)
    any_ = pl.BlockSpec(memory_space=HBM)
    vmem = pl.BlockSpec(memory_space=VMEM)
    smem = pl.BlockSpec(memory_space=pltpu.SMEM)
    sem = lambda *shape: pltpu.SemaphoreType.DMA(shape)
    one = pltpu.SemaphoreType.DMA
    tokens, width = queries.shape

    gathered = pl.pallas_call(
        gather_kernel,
        out_shape=(
            wide(64), wide(64), aux(64), wide(32), wide(32),
            wide(32), wide(32), aux(32), wide(16), wide(16),
            jax.ShapeDtypeStruct((BLK, BLK), jnp.int32),
        ),
        in_specs=[any_] * 5 + [vmem] * 3,
        out_specs=(any_,) * 10 + (vmem,),
        scratch_shapes=[
            VMEM((tokens, width), BF), VMEM((tokens, width), BF), VMEM((HEADS, 8, BLK), F32),
            VMEM((BLK, BLK), F32), VMEM((BLK, BLK), F32),
            sem(2), sem(5), sem(5, 4), sem(5), sem(5), sem(5), sem(5, 4), sem(5), sem(5), sem(5), sem(5), sem(2), sem(2),
            sem(5), sem(5, 4), sem(5), sem(5), sem(2), sem(2),
        ],
        compiler_params=pltpu.CompilerParams(
            collective_id=0, has_side_effects=True, vmem_limit_bytes=16 * 2**20
        ),
        name="gather_blocks",
    )(
        queries, key_rows, value_rows, out_grad, forward_out, log_norm, pattern,
        block_order.reshape(1, BLK),
    )
    table = gathered[-1]

    grads = pl.pallas_call(
        compute_kernel,
        out_shape=(wide(64), wide(32), wide(32), wide(32), wide(16), wide(16)),
        in_specs=[smem] + [vmem] * 10,
        out_specs=(vmem,) * 6,
        scratch_shapes=[VMEM((32 * BLK, BLK), F32), VMEM((32 * BLK, BLK), F32), VMEM((GROUP, BLK), F32)],
        compiler_params=pltpu.CompilerParams(vmem_limit_bytes=56 * 2**20),
        name="block_grads",
    )(table, *gathered[:10])

    flat = jax.ShapeDtypeStruct((tokens, width), BF)
    return pl.pallas_call(
        return_kernel,
        out_shape=(flat, flat, flat),
        in_specs=[vmem] * 6,
        out_specs=(any_,) * 3,
        scratch_shapes=[
            VMEM((2, 16 * BLK, BLK), BF), VMEM((32 * BLK, BLK), BF), VMEM((16 * BLK, BLK), BF),
            VMEM((16 * BLK, BLK), BF), VMEM((3, 16 * BLK, BLK), BF),
            VMEM((16 * BLK, BLK), BF), VMEM((16 * BLK, BLK), BF), VMEM((12 * BLK, BLK), BF),
            VMEM((2, 12 * BLK, BLK), BF), VMEM((3, GROUP, BLK), BF),
            one, sem(2, 4), one, sem(2, 4), one, sem(4), one, one, one, sem(3), one, sem(2, 3), sem(3), sem(3),
        ],
        compiler_params=pltpu.CompilerParams(
            collective_id=1, has_side_effects=True, vmem_limit_bytes=40 * 2**20
        ),
        name="return_grads",
    )(*grads)


def solution(mesh):
    tokens = P(("ctx", "head"), None)
    return jax.shard_map(
        body,
        mesh=mesh,
        in_specs=(tokens,) * 6 + (P(), P()),
        out_specs=(tokens,) * 3,
        check_vma=False,
    )
```

time: 546 us -> 201 us (0.37); the launches traced: 536 us -> 198 us
  matrix products: 204 us -> 0 us
  Pallas kernels: 0 us -> 169 us
  waiting for transfers between devices: 165 us -> 0 us
  local copies, waits for them, and re-layouts: 97 us -> 27.8 us
  starting transfers between devices: 59.7 us -> 0 us
  other arithmetic: 7 us -> 0 us
    dot_general x229 -> x0, matrix products: 204 us -> none  [the longest x90 94.7 us: against_cols(): lax.dot_general(left, right, (((0,), (0,)), ((), ())), preferred_element_...]
    pallas_call x0 -> x3, Pallas kernels: none -> 169 us  [the longest x1 74.3 us: body(): pl.pallas_call(gather_kernel, out_shape=(wide(64), wide(64), aux(64), wid...]
    all_to_all x13 -> x0, waiting for transfers between devices: 165 us -> none  [the longest x1 52.3 us: body(): lax.all_to_all(part_keys, 'ctx', split_axis=0, concat_axis=0, tiled=True)]
    all_to_all x13 -> x0, starting transfers between devices: 59.7 us -> none  [the longest x1 8.47 us: body(): lax.all_to_all(sent_keys, 'ctx', split_axis=0, concat_axis=0, tiled=True)]
    gather x3 -> x0, local copies, waits for them, and re-layouts: 26.8 us -> none  [the longest x2 26.1 us: adjacency(): key_slot = jnp.where(listed >= 0, slot_of[jnp.maximum(listed, 0)], -1)]
    convert_element_type x4 -> x0, local copies, waits for them, and re-layouts: 12.8 us -> none  [the longest x1 6.89 us: body(): sent_values = jnp.einsum('nq,qrw->nrw', owner_map, value_h.reshape(blocks...]
    all_to_all x12 -> x0, local copies, waits for them, and re-layouts: 11.1 us -> none  [the longest x3 3.61 us: body(): lax.all_to_all(value_rows, 'head', split_axis=1, concat_axis=0, tiled=True)]
    another operation x1 -> x0, local copies, waits for them, and re-layouts: 7.82 us -> none  [body(): jnp.stack(value_parts).reshape(groups * blocks_mine, block_len, width)]
  transfers between devices with their start and end apart: 13 -> 0, of which waited for: 11 -> 0; matrix products, arithmetic and copies ran while one was open for 40% -> 0% of each run, Pallas kernels for 0% -> 0%
where the time goes in v1:
time: 201 us; the launch traced here: 198 us
  Pallas kernels  169 us (84%)
  local copies, waits for them, and re-layouts  27.8 us (14%)
    pallas_call x1, Pallas kernels, body(): pl.pallas_call(gather_kernel, out_shape=(wide(64), wide(64), aux(64), wid...  74.3 us
    pallas_call x1, Pallas kernels, body(): pl.pallas_call(compute_kernel, out_shape=(wide(64), wide(32), wide(32), w...  50 us
    pallas_call x1, Pallas kernels, body(): pl.pallas_call(return_kernel, out_shape=(flat, flat, flat), in_specs=[vme...  44.8 us
    unnamed x51, local copies, waits for them, and re-layouts  27.8 us

profile of v1, /device:TPU:32, one launch (start us, length us, event | category | flops | bytes accessed | tf_op | source)
XLA Modules:
  0.0 197.7 jit_solution(1918496746826423743)
XLA Ops:
  0.6 0.8 copy.11.norm_in
  1.4 0.8 copy.12.pat_in
  2.3 0.0 copy-start.10
  2.3 1.1 copy-done.10
  3.4 0.0 copy-start.11
  3.4 1.1 copy-done.11
  4.4 0.0 copy-start.12
  4.4 1.1 copy-done.12
  5.5 0.0 copy-start.13
  5.5 1.1 copy-done.13
  6.6 0.0 copy-start.14
  6.6 1.1 copy-done.14
  7.7 0.0 copy-start.22
  7.7 0.7 copy-done.22
  8.4 74.3 %gather_blocks.1 = (bf16[8192,128]{1,0:T(8,128)(2,1)S(1)}, bf16[8192,128]{1,0:T(8,128)(2,1)S(1)}, f32[64,8,128]{2,1,0:T(8,128)S(1)}, bf16[4096,128]{1,0:T(8,128)...) custom-call(bf16[128,2560]{1,0:T(8,128)(2,1)S(1)} %copy-done.10, ...), custom_call_target="tpu_custom_call" | custom-call | tf_op jit(solution)/shard_map/gather_blocks/pallas_call | solution.py:457
  82.7 0.0 copy-start.1
  82.7 1.3 copy-done.1
  84.0 0.0 copy-start.2
  84.0 1.3 copy-done.2
  85.3 0.0 copy-start.3
  85.3 1.0 copy-done.3
  86.3 0.0 copy-start.4
  86.3 1.1 copy-done.4
  87.4 0.0 copy-start.5
  87.4 1.1 copy-done.5
  88.4 0.0 copy-start.6
  88.4 1.0 copy-done.6
  89.4 0.0 copy-start.17
  89.4 0.8 copy-done.17
  90.2 0.0 copy-start.18
  90.2 0.8 copy-done.18
  91.0 0.0 copy-start.19
  91.0 0.7 copy-done.19
  91.7 0.0 copy-start.20
  91.7 0.7 copy-done.20
  92.4 0.0 copy-start.21
  92.4 0.6 copy-done.21
  93.0 50.0 %block_grads.1 = (bf16[8192,128]{1,0:T(8,128)(2,1)}, bf16[4096,128]{1,0:T(8,128)(2,1)}, bf16[4096,128]{1,0:T(8,128)(2,1)}, bf16[4096,128]{1,0:T(8,128)(2,1)}, bf...) custom-call(s32[128,128]{1,0:T(8,128)} %copy-done.21, bf16[8192,128]{1,0:T(8,128)(2,1)} %copy-done.1, ...), custom_call_target="tpu_custom_call" | custom-call | tf_op jit(solution)/shard_map/block_grads/pallas_call | solution.py:482
  143.0 0.0 copy-start
  143.0 1.6 copy-done
  144.6 0.0 copy-start.7
  144.6 1.2 copy-done.7
  145.8 0.0 copy-start.8
  145.8 1.2 copy-done.8
  147.0 0.0 copy-start.9
  147.0 1.2 copy-done.9
  148.3 0.0 copy-start.15
  148.3 1.0 copy-done.15
  149.3 0.0 copy-start.16
  149.3 1.0 copy-done.16
  150.3 44.8 %return_grads.1 = (bf16[128,2560]{1,0:T(8,128)(2,1)S(1)}, bf16[128,2560]{1,0:T(8,128)(2,1)S(1)}, bf16[128,2560]{1,0:T(8,128)(2,1)S(1)}) custom-call(bf16[8192,128]{1,0:T(8,128)(2,1)S(1)} %copy-done, bf16[4096,128]{1,0:T(8,128)(2,1)S(1)} %copy-done.7, bf16[4096,128]{1,0:T(8,128)(2,1)S(1)} %copy-done.8, bf16[4096,128]{1,0:T(8,128)(2,1)S(1)} %copy-done.9, ...), custom_call_target="tpu_custom_call" | custom-call | tf_op jit(solution)/shard_map/return_grads/pallas_call | solution.py:493
  195.2 0.8 copy.16
  196.0 0.8 copy.17
  196.8 0.8 copy.18
Async XLA Ops:
  2.3 1.1 copy-start.10
  3.4 1.1 copy-start.11
  4.4 1.1 copy-start.12
  5.5 1.1 copy-start.13
  6.6 1.1 copy-start.14
  7.7 0.7 copy-start.22
  82.7 1.3 copy-start.1
  84.0 1.3 copy-start.2
  85.3 1.0 copy-start.3
  86.3 1.1 copy-start.4
  87.4 1.1 copy-start.5
  88.4 1.0 copy-start.6
  89.4 0.8 copy-start.17
  90.2 0.8 copy-start.18
  91.0 0.7 copy-start.19
  91.7 0.7 copy-start.20
  92.4 0.6 copy-start.21
  143.0 1.6 copy-start
  144.6 1.2 copy-start.7
  145.8 1.2 copy-start.8
  147.0 1.2 copy-start.9
  148.3 1.0 copy-start.15
  149.3 1.0 copy-start.16

commit v2 on v1

v2 whole, which is shorter than its diff:
```python
import functools

import jax
import jax.numpy as jnp
from jax import lax
from jax.experimental import pallas as pl
from jax.experimental.pallas import tpu as pltpu
from jax.sharding import PartitionSpec as P

MESH = pl.DeviceIdType.MESH
HBM = pl.ANY
VMEM = pltpu.VMEM
BF = jnp.bfloat16
F32 = jnp.float32
BLK = 128
HEADS = 20
LOG2E = 1.4426950408889634
SCALE = 128 ** -0.5
FAR = 1e30
GROUP = 4 * BLK
VMEM_LIMIT = 60 * 2**20


def coords():
    c = lax.axis_index("ctx")
    return c // 8, (c // 2) % 4, c % 2, lax.axis_index("head")


def dev(x, z, k, y):
    return (x * 8 + z * 2 + k, y)


def rows(start, size):
    return pl.ds(pl.multiple_of(start, BLK), size)


def cols(head):
    return pl.ds(pl.multiple_of(head * BLK, BLK), BLK)


def q_pair(z):
    return z + 1 - 2 * (z % 2)


def k_pair(z):
    return (z + 3 + 2 * (z % 2)) % 4


def send(src, dst, ss, rs, to):
    pltpu.make_async_remote_copy(
        src_ref=src, dst_ref=dst, send_sem=ss, recv_sem=rs, device_id=to, device_id_type=MESH
    ).start()


def wait(ref, sem):
    pltpu.make_async_copy(ref, ref, sem).wait()


def greet():
    x, z, k, y = coords()
    barrier = pltpu.get_barrier_semaphore()
    peers = [dev((x + dx) % 4, z, k, (y + dy) % 4) for dx in range(4) for dy in range(4) if dx or dy]
    peers += [dev(x, (z + dz) % 4, k, y) for dz in range(1, 4)]
    peers.append(dev(x, z, 1 - k, y))
    for peer in peers:
        pl.semaphore_signal(barrier, inc=1, device_id=peer, device_id_type=MESH)
    pl.semaphore_wait(barrier, len(peers))


DX = (0, 1, 3, 2)
AHEAD = 6
BSTEP = 3


def gather_kernel(
    q_in, k_in, v_in, g_in, o_in, norm_in, pat_in, order_in,
    qa, ga, xa, ka, va, qb, gb, xb, kb, vb, table,
    g_v, o_v, aux, pat_v,
    load_sem, sa1, ra1, sb1, rb1, s_zq, r_zq, s_c, r_c, s_c2, r_c2, s_zk, r_zk,
    s_bz, r_bz, s_bc, r_bc, s_bx, r_bx,
):
    x, z, k, y = coords()
    load_g = pltpu.make_async_copy(g_in, g_v, load_sem.at[0])
    load_o = pltpu.make_async_copy(o_in, o_v, load_sem.at[1])
    load_g.start()
    load_o.start()
    greet()
    mine = (x * 4 + y) * BLK

    slot = k * 4 + z
    wide = {0: (q_in, qa, qb), 1: (g_in, ga, gb), 2: (k_in, ka, kb), 3: (v_in, va, vb), 4: (aux, xa, xb)}

    def cut(a, head):
        src = wide[a][0]
        return src.at[head] if a == 4 else src.at[:, cols(head)]

    def scatter_a(a, wave):
        dst = xa.at[x * 4 + y] if a == 4 else wide[a][1].at[rows(mine, BLK), :]
        for dx in range(4):
            dy = (dx + wave) % 4
            tx, ty = (x + dx) % 4, (y + dy) % 4
            src = cut(a, ty * 4 + tx)
            if dx or dy:
                send(src, dst, sa1.at[a], ra1.at[a, wave], dev(tx, z, k, ty))
            else:
                pltpu.make_async_copy(src, dst, ra1.at[a, wave]).start()

    def scatter_b(a):
        if a == 4:
            dst = xb.at[slot * 4 + y]
        else:
            dst = wide[a][2].at[rows((slot if a < 2 else x) * GROUP + y * BLK, BLK), :]
        for dy in range(4):
            ty = (y + dy) % 4
            if dy:
                send(cut(a, 16 + ty), dst, sb1.at[a], rb1.at[a], dev(x, z, k, ty))
            else:
                pltpu.make_async_copy(cut(a, 16 + ty), dst, rb1.at[a]).start()

    steps = [(a, wave) for wave in range(4) for a in (0, 2, 1, 3)]
    for a in (0, 2, 1, 3):
        scatter_b(a)
    for step in steps[:AHEAD]:
        scatter_a(*step)

    load_g.wait()
    load_o.wait()
    for h in range(HEADS):
        prod = g_v[:, h * BLK:(h + 1) * BLK].astype(F32) * o_v[:, h * BLK:(h + 1) * BLK].astype(F32)
        dot = jnp.sum(prod.T, axis=0, keepdims=True)
        aux[h] = jnp.concatenate([norm_in[h:h + 1] * LOG2E, dot, jnp.zeros((6, BLK), F32)], axis=0)

    for wave in range(4):
        scatter_a(4, wave)
    scatter_b(4)

    def part(a, ref, quad, wave, dx):
        at = (quad * 4 + (x + 4 - dx) % 4) * 4 + (y + 8 - dx - wave) % 4
        return ref.at[pl.ds(at, 1)] if a == 4 else ref.at[rows(at * BLK, BLK), :]

    def whole(a, ref, count=4):
        return ref.at[pl.ds(0, count)] if a == 4 else ref.at[pl.ds(0, count * BLK), :]

    buf_a = {0: qa, 1: ga, 2: ka, 3: va, 4: xa}
    buf_b = {0: qb, 1: gb, 2: kb, 3: vb, 4: xb}
    to_q = dev(x, q_pair(z), k, y)
    to_k = dev(x, k_pair(z), k, y)
    to_c = dev(x, z, 1 - k, y)

    def forward_a(a, wave):
        ref = buf_a[a]
        wait(whole(a, ref), ra1.at[a, wave])
        for dx in range(4):
            own, there = part(a, ref, 0, wave, dx), part(a, ref, 1, wave, dx)
            if a in (2, 3):
                send(own, there, s_zk.at[a - 2], r_zk.at[a - 2], to_k)
            else:
                send(own, there, s_zq.at[a], r_zq.at[a, wave], to_q)
                send(own, part(a, ref, 2, wave, dx), s_c.at[a], r_c.at[a], to_c)

    def slab(a, ref, index, count=1):
        if a == 4:
            return ref.at[pl.ds(index * 4, 4 * count)]
        return ref.at[rows(index * GROUP, GROUP * count), :]

    def forward_b():
        for a in (0, 1, 4):
            ref = buf_b[a]
            own = slab(a, ref, slot)
            wait(own, rb1.at[a])
            for dz in (1, 3, 2):
                send(own, own, s_bz.at[a], r_bz.at[a, dz], dev(x, (z + dz) % 4, k, y))
            send(own, own, s_bc.at[a], r_bc.at[a], to_c)
        for a in (2, 3):
            ref = buf_b[a]
            own = slab(a, ref, x)
            wait(own, rb1.at[a])
            for dx in (1, 3, 2):
                send(own, own, s_bx.at[a - 2], r_bx.at[a - 2], dev((x + dx) % 4, z, k, y))

    for n, step in enumerate(steps):
        if n == BSTEP:
            forward_b()
        forward_a(*step)
        if n + AHEAD < 16:
            scatter_a(*steps[n + AHEAD])
    for wave in range(4):
        forward_a(4, wave)

    pat_v[...] = jnp.full((BLK, BLK), -1.0, F32)
    pat_v[0:36, :] = pat_in[...].astype(F32)
    order = jnp.broadcast_to(order_in[...].astype(F32), (BLK, BLK))
    i0 = lax.broadcasted_iota(jnp.int32, (BLK, BLK), 0)
    i1 = lax.broadcasted_iota(jnp.int32, (BLK, BLK), 1)
    hot = jnp.where(i0.astype(F32) == order, 1.0, 0.0)
    pat_v[...] = jnp.dot(pat_v[...].astype(BF), hot.astype(BF), preferred_element_type=F32)
    order_t = order.T
    adj = jnp.zeros((BLK, BLK), F32)
    for e in range(36):
        adj = jnp.where(pat_v[e:e + 1, :] == order_t, 1.0, adj)
    adj = adj.T
    local = (i0 // 4) == (i1 // 4)
    pick = jnp.where((i0 // 4) == i1, (i0 % 4 + 1).astype(F32), 0.0)
    own_cols = jnp.where(i1 == 32 + i0 % 4, 1.0, 0.0)
    table[...] = (
        jnp.dot(jnp.where(local, 0.0, adj).astype(BF), pick.astype(BF), preferred_element_type=F32)
        + jnp.dot(jnp.where(local, adj, 0.0).astype(BF), own_cols.astype(BF), preferred_element_type=F32)
    ).astype(jnp.int32)

    for dz in (1, 3, 2):
        for a in (0, 1, 4):
            ref = buf_b[a]
            got = slab(a, ref, k * 4 + (z + 4 - dz) % 4)
            wait(got, r_bz.at[a, dz])
            send(got, got, s_bc.at[a], r_bc.at[a], to_c)
    for wave in range(4):
        for a in (0, 1, 4):
            ref = buf_a[a]
            wait(whole(a, ref), r_zq.at[a, wave])
            for dx in range(4):
                send(part(a, ref, 1, wave, dx), part(a, ref, 3, wave, dx), s_c2.at[a], r_c2.at[a], to_c)

    def quad(a, ref, index):
        if a == 4:
            return ref.at[pl.ds(index * 16, 16)]
        return ref.at[pl.ds(index * 4 * GROUP, 4 * GROUP), :]

    for a in (2, 3):
        wait(quad(a, buf_a[a], 1), r_zk.at[a - 2])
        wait(quad(a, buf_a[a], 0), s_zk.at[a - 2])
        wait(slab(a, buf_b[a], 0, 3), r_bx.at[a - 2])
        wait(slab(a, buf_b[a], 0, 3), s_bx.at[a - 2])
    for a in (0, 1, 4):
        wait(quad(a, buf_a[a], 2), r_c.at[a])
        wait(quad(a, buf_a[a], 3), r_c2.at[a])
        wait(quad(a, buf_a[a], 0), s_zq.at[a])
        wait(quad(a, buf_a[a], 0), s_c.at[a])
        wait(quad(a, buf_a[a], 0), s_c2.at[a])
        wait(slab(a, buf_b[a], 0, 4), r_bc.at[a])
        wait(slab(a, buf_b[a], 0, 4), s_bc.at[a])
        wait(slab(a, buf_b[a], 0, 3), s_bz.at[a])
    for a in range(5):
        ref = buf_a[a]
        if a == 4:
            wait(ref.at[pl.ds(0, 15)], sa1.at[a])
            wait(ref.at[pl.ds(0, 3)], sb1.at[a])
        else:
            wait(ref.at[pl.ds(0, 15 * BLK), :], sa1.at[a])
            wait(ref.at[pl.ds(0, 3 * BLK), :], sb1.at[a])


def compute_kernel(
    table, qa_in, ga_in, xa_in, ka_in, va_in, qb_in, gb_in, xb_in, kb_in, vb_in,
    dqa_out, dka_out, dva_out, dqb_out, dkb_out, dvb_out,
    qa, ga, xa, ka, va, qb, gb, xb, kb, vb, dqa, dka, dva, dqb, dkb, dvb, in_sem, out_sem,
    acc_k, acc_v, kt_ref, s_ref, d_ref, p_ref, e_ref,
):
    x, z, k, y = coords()
    base2 = SCALE * LOG2E
    zq, zk = q_pair(z), k_pair(z)
    pairs_in = [
        (ka_in, ka), (va_in, va), (qa_in, qa), (ga_in, ga), (xa_in, xa),
        (kb_in, kb), (vb_in, vb), (qb_in, qb), (gb_in, gb), (xb_in, xb),
    ]
    loads = [pltpu.make_async_copy(src, dst, in_sem.at[i]) for i, (src, dst) in enumerate(pairs_in)]
    for load in loads:
        load.start()
    stores = []

    def store(src, dst):
        copy = pltpu.make_async_copy(src, dst, out_sem.at[len(stores)])
        copy.start()
        stores.append(copy)

    def lanes(x_ref, q, row):
        return jnp.concatenate([x_ref[q * 4 + b, row:row + 1, :] for b in range(4)], axis=1)

    def blocks(ref, places, axis=0):
        return jnp.concatenate([ref[pl.ds(p, BLK), :] for p in places], axis=axis)

    def span(q):
        return pl.ds(pl.multiple_of(q * GROUP, GROUP), GROUP)

    def picked(c, groups):
        places, biases = [], []
        for first, key_index in groups:
            for i in range(4):
                code = table[4 * c, key_index(i)]
                places.append(pl.multiple_of((first + i) * GROUP + jnp.maximum(code - 1, 0) * BLK, BLK))
                biases.append(jnp.where(code > 0, 0.0, FAR))
        return places, biases

    def soften(score, dprob, norm, dot, hide=None):
        prob = jnp.exp2(score * base2 - norm)
        if hide is not None:
            prob = jnp.where(hide, 0.0, prob)
        return prob.astype(BF), (prob * (dprob - dot)).astype(BF)

    def stage_1(q_ref, g_ref, k_ref, v_ref, q, places, s, d):
        s[...] = jnp.dot(blocks(k_ref, places), q_ref[span(q), :].T, preferred_element_type=F32)
        d[...] = jnp.dot(blocks(v_ref, places), g_ref[span(q), :].T, preferred_element_type=F32)

    def stage_2(x_ref, q, biases, s, d, p, e):
        norm, dot = lanes(x_ref, q, 0), lanes(x_ref, q, 1)
        for i, bias in enumerate(biases):
            cut = slice(i * BLK, (i + 1) * BLK)
            p[cut, :], e[cut, :] = soften(s[cut, :], d[cut, :], norm + bias, dot)

    def stage_3(q_ref, g_ref, dq_ref, q, places, p, e):
        dk = jnp.dot(e[...], q_ref[span(q), :], preferred_element_type=F32)
        dv = jnp.dot(p[...], g_ref[span(q), :], preferred_element_type=F32)
        dq = jnp.dot(blocks(kt_ref, places, 1), e[...], preferred_element_type=F32)
        for i, at in enumerate(places):
            acc_k[pl.ds(at, BLK), :] += dk[i * BLK:(i + 1) * BLK]
            acc_v[pl.ds(at, BLK), :] += dv[i * BLK:(i + 1) * BLK]
        dq_ref[span(q), :] = (dq * SCALE).T.astype(BF)

    def turn(k_ref, n):
        def step(i, carry):
            at = pl.ds(pl.multiple_of(i * BLK, BLK), BLK)
            kt_ref[at, :] = k_ref[at, :].T
            return carry

        lax.fori_loop(0, n, step, 0)

    def finish(dk_ref, dv_ref, n):
        def step(i, carry):
            at = span(i)
            dk_ref[at, :] = (acc_k[at, :] * SCALE).astype(BF)
            dv_ref[at, :] = acc_v[at, :].astype(BF)
            acc_k[at, :] = jnp.zeros((GROUP, BLK), F32)
            acc_v[at, :] = jnp.zeros((GROUP, BLK), F32)
            return carry

        lax.fori_loop(0, n, step, 0)

    def main(q_ref, g_ref, x_ref, k_ref, v_ref, dq_ref, count, c_of, groups):
        n = len(groups) * GROUP
        s, d = s_ref.at[:, 0:n, :], d_ref.at[:, 0:n, :]
        p, e = p_ref.at[:, 0:n, :], e_ref.at[:, 0:n, :]

        def one(t, half, stages):
            now, then = half, 1 - half
            if 3 in stages:
                places3, _ = picked(c_of(t - 2), groups)
                stage_3(q_ref, g_ref, dq_ref, t - 2, places3, p.at[now], e.at[now])
            if 1 in stages:
                places1, _ = picked(c_of(t), groups)
                stage_1(q_ref, g_ref, k_ref, v_ref, t, places1, s.at[now], d.at[now])
            if 2 in stages:
                _, biases2 = picked(c_of(t - 1), groups)
                stage_2(x_ref, t - 1, biases2, s.at[then], d.at[then], p.at[then], e.at[then])

        def step(it, carry):
            for half in range(2):
                one(2 * it + half, half, (1, 2, 3))
            return carry

        one(0, 0, (1,))
        one(1, 1, (1, 2))
        lax.fori_loop(1, count // 2, step, 0)
        one(count, 0, (2, 3))
        one(count + 1, 1, (3,))

    def diag(q_ref, g_ref, x_ref, k_ref, v_ref, dq_ref, q, c, own):
        here = span(own)
        places = [pl.multiple_of(own * GROUP + b * BLK, BLK) for b in range(4)]
        query, grad = q_ref[span(q), :], g_ref[span(q), :]
        score = jnp.dot(k_ref[here, :], query.T, preferred_element_type=F32)
        dprob = jnp.dot(v_ref[here, :], grad.T, preferred_element_type=F32)
        norm, dot = lanes(x_ref, q, 0), lanes(x_ref, q, 1)
        probs, scores = [], []
        key_at = lax.broadcasted_iota(jnp.int32, (BLK, GROUP), 0)
        query_at = lax.broadcasted_iota(jnp.int32, (BLK, GROUP), 1)
        for i in range(4):
            bias = jnp.concatenate(
                [
                    jnp.full((1, BLK), jnp.where(table[4 * c + b, 32 + i] > 0, 0.0, FAR), F32)
                    for b in range(4)
                ],
                axis=1,
            )
            hide = (query_at >= i * BLK) & (query_at < key_at + i * BLK)
            cut = slice(i * BLK, (i + 1) * BLK)
            prob, score_e = soften(score[cut], dprob[cut], norm + bias, dot, hide)
            probs.append(prob)
            scores.append(score_e)
        prob = jnp.concatenate(probs, axis=0)
        score = jnp.concatenate(scores, axis=0)
        acc_k[here, :] += jnp.dot(score, query, preferred_element_type=F32)
        acc_v[here, :] += jnp.dot(prob, grad, preferred_element_type=F32)
        dq = jnp.dot(blocks(kt_ref, places, 1), score, preferred_element_type=F32)
        dq_ref[span(q), :] = (dq_ref[span(q), :].astype(F32) + (dq * SCALE).T).astype(BF)

    acc_k[...] = jnp.zeros_like(acc_k)
    acc_v[...] = jnp.zeros_like(acc_v)

    def index_a(q):
        quad, xq = q // 4, q % 4
        zc = jnp.where(quad % 2 == 0, z, zq)
        kc = jnp.where(quad < 2, k, 1 - k)
        return xq * 8 + zc * 2 + kc

    loads[0].wait()
    turn(ka, 32)
    for load in loads[1:5]:
        load.wait()
    main(qa, ga, xa, ka, va, dqa, 16, index_a, [(0, lambda i: i * 8 + z * 2 + k), (4, lambda i: i * 8 + zk * 2 + k)])

    late = pl.ds(4 * GROUP, 12 * GROUP)
    store(dqa.at[late, :], dqa_out.at[late, :])

    def diag_a(q, carry):
        diag(qa, ga, xa, ka, va, dqa, q, index_a(q), q)
        return carry

    lax.fori_loop(0, 4, diag_a, 0)
    early = pl.ds(0, 4 * GROUP)
    store(dqa.at[early, :], dqa_out.at[early, :])
    finish(dka, dva, 8)
    store(dka, dka_out)
    store(dva, dva_out)
    for load in loads[5:]:
        load.wait()

    turn(kb, 16)
    main(qb, gb, xb, kb, vb, dqb, 8, lambda q: x * 8 + (q % 4) * 2 + q // 4, [(0, lambda i: i * 8 + z * 2 + k)])
    diag(qb, gb, xb, kb, vb, dqb, k * 4 + z, x * 8 + z * 2 + k, x)
    store(dqb, dqb_out)
    finish(dkb, dvb, 4)
    store(dkb, dkb_out)
    store(dvb, dvb_out)
    for copy in stores:
        copy.wait()


def compute_call(table, *gathered):
    wide = lambda n: jax.ShapeDtypeStruct((n * BLK, BLK), BF)
    any_ = pl.BlockSpec(memory_space=HBM)
    hold = lambda n: VMEM((n * BLK, BLK), BF)
    aux = lambda n: VMEM((n, 8, BLK), F32)
    return pl.pallas_call(
        compute_kernel,
        out_shape=(wide(64), wide(32), wide(32), wide(32), wide(16), wide(16)),
        in_specs=[pl.BlockSpec(memory_space=pltpu.SMEM)] + [any_] * 10,
        out_specs=(any_,) * 6,
        scratch_shapes=[
            hold(64), hold(64), aux(64), hold(32), hold(32), hold(32), hold(32), aux(32), hold(16), hold(16),
            hold(64), hold(32), hold(32), hold(32), hold(16), hold(16),
            pltpu.SemaphoreType.DMA((10,)), pltpu.SemaphoreType.DMA((7,)),
            VMEM((32 * BLK, BLK), F32), VMEM((32 * BLK, BLK), F32), hold(32),
            VMEM((2, 8 * BLK, GROUP), F32), VMEM((2, 8 * BLK, GROUP), F32),
            VMEM((2, 8 * BLK, GROUP), BF), VMEM((2, 8 * BLK, GROUP), BF),
        ],
        compiler_params=pltpu.CompilerParams(vmem_limit_bytes=VMEM_LIMIT),
        name="block_grads",
    )(table, *gathered)


def return_kernel(
    dqa, dka, dva, dqb, dkb, dvb,
    dq_out, dk_out, dv_out,
    own_q, own_k, own_v, own_bq, own_bk, own_bv, own_sem,
    got_zk, got_c, got_zq, put_zq, fin, bgot_c, bput_q, bgot_z, bgot_x, bfin,
    s_zk, r_zk, s_c, r_c, s_zq, r_zq, s_bc, r_bc, s_bz, r_bz, s_bx, r_bx, s_out, r_out,
):
    x, z, k, y = coords()
    outs = (dq_out, dk_out, dv_out)
    to_q = dev(x, q_pair(z), k, y)
    to_k = dev(x, k_pair(z), k, y)
    to_c = dev(x, z, 1 - k, y)
    half, quarter = pl.ds(0, 4 * GROUP), rows(x * GROUP, GROUP)
    loads = [
        pltpu.make_async_copy(src, dst, own_sem.at[i])
        for i, (src, dst) in enumerate([
            (dqa.at[pl.ds(0, 8 * GROUP), :], own_q),
            (dqb.at[rows(k * 4 * GROUP, 4 * GROUP), :], own_bq),
            (dka.at[half, :], own_k), (dva.at[half, :], own_v),
            (dkb.at[quarter, :], own_bk), (dvb.at[quarter, :], own_bv),
        ])
    ]
    for load in loads:
        load.start()
    greet()

    def chunk(ref, quad, dx):
        return ref.at[rows((quad * 4 + (x + dx) % 4) * GROUP, GROUP), :]

    def slab(ref, index):
        return ref.at[rows(index * GROUP, GROUP), :]

    for dx in DX:
        send(chunk(dqa, 3, dx), chunk(got_c, 1, dx), s_c, r_c.at[1, dx], to_c)
    send(dqb.at[rows((1 - k) * 4 * GROUP, 4 * GROUP), :], bgot_c, s_bc, r_bc, to_c)
    for dx in DX:
        for n, src in enumerate((dka, dva)):
            send(chunk(src, 1, dx), chunk(got_zk.at[n], 0, dx), s_zk, r_zk.at[n, dx], to_k)
    for dx in DX:
        send(chunk(dqa, 2, dx), chunk(got_c, 0, dx), s_c, r_c.at[0, dx], to_c)
    for dx in (1, 3, 2):
        for n, src in enumerate((dkb, dvb)):
            send(slab(src, (x + dx) % 4), slab(bgot_x.at[n], dx - 1), s_bx, r_bx.at[n, dx - 1], dev((x + dx) % 4, z, k, y))

    def add(*refs):
        total = refs[0][...].astype(F32)
        for ref in refs[1:]:
            total = total + ref[...].astype(F32)
        return total.astype(BF)

    for load in loads:
        load.wait()

    for dx in DX:
        wait(chunk(got_c, 1, dx), r_c.at[1, dx])
        part = chunk(put_zq, 0, dx)
        part[...] = add(chunk(own_q, 1, dx), chunk(got_c, 1, dx))
        send(part, chunk(got_zq, 0, dx), s_zq, r_zq.at[dx], to_q)
    wait(bgot_c, r_bc)
    for dz in (1, 3, 2):
        zt = (z + dz) % 4
        part = slab(bput_q, zt)
        part[...] = add(slab(own_bq, zt), slab(bgot_c, zt))
        send(part, slab(bgot_z, dz - 1), s_bz, r_bz.at[dz - 1], dev(x, zt, k, y))

    def give(n, src, base, tx, head_of, dx):
        for dy in range(4):
            ty = (y + dy) % 4
            block = src.at[rows(base + ty * BLK, BLK), :]
            dst = outs[n].at[:, cols(head_of)]
            if dx or dy:
                send(block, dst, s_out.at[n], r_out.at[n], dev(tx, z, k, ty))
            else:
                pltpu.make_async_copy(block, dst, r_out.at[n]).start()

    for dx in (1, 3, 2, 0):
        tx = (x + dx) % 4
        for n, own in ((1, own_k), (2, own_v)):
            wait(chunk(got_zk.at[n - 1], 0, dx), r_zk.at[n - 1, dx])
            out = chunk(fin.at[n], 0, dx)
            out[...] = add(chunk(own, 0, dx), chunk(got_zk.at[n - 1], 0, dx))
            give(n, fin.at[n], tx * GROUP, tx, y * 4 + x, dx)
    for dx in (1, 3, 2, 0):
        tx = (x + dx) % 4
        wait(chunk(got_c, 0, dx), r_c.at[0, dx])
        wait(chunk(got_zq, 0, dx), r_zq.at[dx])
        out = chunk(fin.at[0], 0, dx)
        out[...] = add(chunk(own_q, 0, dx), chunk(got_c, 0, dx), chunk(got_zq, 0, dx))
        give(0, fin.at[0], tx * GROUP, tx, y * 4 + x, dx)
    for n, own in ((1, own_bk), (2, own_bv)):
        for i in range(3):
            wait(slab(bgot_x.at[n - 1], i), r_bx.at[n - 1, i])
        bfin[n] = add(own, *[slab(bgot_x.at[n - 1], i) for i in range(3)])
        give(n, bfin.at[n], 0, x, 16 + y, 0)
    for i in range(3):
        wait(slab(bgot_z, i), r_bz.at[i])
    bfin[0] = add(slab(own_bq, z), slab(bgot_c, z), *[slab(bgot_z, i) for i in range(3)])
    give(0, bfin.at[0], 0, x, 16 + y, 0)

    for n in range(3):
        wait(outs[n], r_out.at[n])
        wait(dqa.at[pl.ds(0, 18 * BLK), :], s_out.at[n])
    wait(dqa.at[pl.ds(0, 8 * GROUP), :], s_c)
    wait(dqa.at[pl.ds(0, 8 * GROUP), :], s_zk)
    wait(put_zq, s_zq)
    wait(bgot_c, s_bc)
    wait(bgot_z, s_bz)
    wait(dqa.at[pl.ds(0, 6 * GROUP), :], s_bx)


def body(queries, key_rows, value_rows, forward_out, out_grad, log_norm, block_order, pattern):
    wide = lambda n: jax.ShapeDtypeStruct((n * BLK, BLK), BF)
    aux = lambda n: jax.ShapeDtypeStruct((n, 8, BLK), F32)
    any_ = pl.BlockSpec(memory_space=HBM)
    vmem = pl.BlockSpec(memory_space=VMEM)
    sem = lambda *shape: pltpu.SemaphoreType.DMA(shape)
    one = pltpu.SemaphoreType.DMA
    hold = lambda n: VMEM((n * BLK, BLK), BF)
    tokens, width = queries.shape

    gathered = pl.pallas_call(
        gather_kernel,
        out_shape=(
            wide(64), wide(64), aux(64), wide(32), wide(32),
            wide(32), wide(32), aux(32), wide(16), wide(16),
            jax.ShapeDtypeStruct((BLK, BLK), jnp.int32),
        ),
        in_specs=[any_] * 5 + [vmem] * 3,
        out_specs=(any_,) * 10 + (vmem,),
        scratch_shapes=[
            VMEM((tokens, width), BF), VMEM((tokens, width), BF), VMEM((HEADS, 8, BLK), F32),
            VMEM((BLK, BLK), F32),
            sem(2), sem(5), sem(5, 4), sem(5), sem(5), sem(5), sem(5, 4), sem(5), sem(5), sem(5), sem(5), sem(2), sem(2),
            sem(5), sem(5, 4), sem(5), sem(5), sem(2), sem(2),
        ],
        compiler_params=pltpu.CompilerParams(
            collective_id=0, has_side_effects=True, vmem_limit_bytes=VMEM_LIMIT
        ),
        name="gather_blocks",
    )(
        queries, key_rows, value_rows, out_grad, forward_out, log_norm.T, pattern.T,
        block_order.reshape(1, BLK),
    )
    table = gathered[-1]

    grads = compute_call(table, *gathered[:10])
    flat = jax.ShapeDtypeStruct((tokens, width), BF)
    return pl.pallas_call(
        return_kernel,
        out_shape=(flat, flat, flat),
        in_specs=[any_] * 6,
        out_specs=(any_,) * 3,
        scratch_shapes=[
            hold(32), hold(16), hold(16), hold(16), hold(4), hold(4), sem(6),
            VMEM((2, 16 * BLK, BLK), BF), VMEM((32 * BLK, BLK), BF), VMEM((16 * BLK, BLK), BF),
            VMEM((16 * BLK, BLK), BF), VMEM((3, 16 * BLK, BLK), BF),
            VMEM((16 * BLK, BLK), BF), VMEM((16 * BLK, BLK), BF), VMEM((12 * BLK, BLK), BF),
            VMEM((2, 12 * BLK, BLK), BF), VMEM((3, GROUP, BLK), BF),
            one, sem(2, 4), one, sem(2, 4), one, sem(4), one, one, one, sem(3), one, sem(2, 3), sem(3), sem(3),
        ],
        compiler_params=pltpu.CompilerParams(
            collective_id=1, has_side_effects=True, vmem_limit_bytes=VMEM_LIMIT
        ),
        name="return_grads",
    )(*grads)


def solution(mesh):
    tokens = P(("ctx", "head"), None)
    return jax.shard_map(
        body,
        mesh=mesh,
        in_specs=(tokens,) * 6 + (P(), P()),
        out_specs=(tokens,) * 3,
        check_vma=False,
    )
```

time: 201 us -> 159 us (0.79); the launches traced: 198 us -> 158 us
  local copies, waits for them, and re-layouts: 27.8 us -> 4.84 us
  Pallas kernels: 169 us -> 152 us
    unnamed x51 -> x5, local copies, waits for them, and re-layouts: 27.8 us -> 4.84 us
    pallas_call x1, Pallas kernels: 74.3 us -> 59.1 us  [body(): pl.pallas_call(gather_kernel, out_shape=(wide(64), wide(64), aux(64), wid...]
where the time goes in v2:
time: 159 us; the launch traced here: 158 us
  Pallas kernels  152 us (96%)
  local copies, waits for them, and re-layouts  4.84 us (3%)
    pallas_call x1, Pallas kernels, body(): pl.pallas_call(gather_kernel, out_shape=(wide(64), wide(64), aux(64), wid...  59.1 us
    pallas_call x1, Pallas kernels, body(): pl.pallas_call(return_kernel, out_shape=(flat, flat, flat), in_specs=[any...  51.4 us
    pallas_call x1, Pallas kernels, compute_call(): pl.pallas_call(compute_kernel, out_shape=(wide(64), wide(32), wide(32), w...  41.8 us
    unnamed x5, local copies, waits for them, and re-layouts  4.84 us

profile of v2, /device:TPU:32, one launch (start us, length us, event | category | flops | bytes accessed | tf_op | source)
XLA Modules:
  0.0 157.8 jit_solution(9841497491876853455)
XLA Ops:
  0.6 59.1 %gather_blocks.1 = (bf16[8192,128]{1,0:T(8,128)(2,1)}, bf16[8192,128]{1,0:T(8,128)(2,1)}, f32[64,8,128]{2,1,0:T(8,128)}, bf16[4096,128]{1,0:T(8,128)(2,1)}, bf16...) custom-call(bf16[128,2560]{1,0:T(8,128)(2,1)} %q_in.1, ...), custom_call_target="tpu_custom_call" | custom-call | tf_op jit(solution)/shard_map/gather_blocks/pallas_call | solution.py:580
  59.7 41.8 %block_grads.1 = (bf16[8192,128]{1,0:T(8,128)(2,1)}, bf16[4096,128]{1,0:T(8,128)(2,1)}, bf16[4096,128]{1,0:T(8,128)(2,1)}, bf16[4096,128]{1,0:T(8,128)(2,1)}, bf...) custom-call(s32[128,128]{1,0:T(8,128)} %get-tuple-element.20.table, bf16[8192,128]{1,0:T(8,128)(2,1)} %get-tuple-element.21.qa_in, ...), custom_call_target="tpu_custom_call" | custom-call | tf_op jit(solution)/shard_map/block_grads/pallas_call | solution.py:442
  101.6 51.4 %return_grads.1 = (bf16[128,2560]{1,0:T(8,128)(2,1)}, bf16[128,2560]{1,0:T(8,128)(2,1)}, bf16[128,2560]{1,0:T(8,128)(2,1)}) custom-call(bf16[8192,128]{1,0:T(8,128)(2,1)} %get-tuple-element.31.dqa, bf16[4096,128]{1,0:T(8,128)(2,1)} %get-tuple-element.32.dka, bf16[4096,128]{1,0:T(8,128)(2,1)} %get-tuple-element.33.dva, ...), custom_call_target="tpu_custom_call" | custom-call | tf_op jit(solution)/shard_map/return_grads/pallas_call | solution.py:607
  153.0 0.0 copy-start
  153.0 2.0 %copy.14 = bf16[128,2560]{1,0:T(8,128)(2,1)} copy(bf16[128,2560]{1,0:T(8,128)(2,1)} %get-tuple-element.40) | data formatting | bytes 1310720
  155.0 2.0 %copy.15 = bf16[128,2560]{1,0:T(8,128)(2,1)} copy(bf16[128,2560]{1,0:T(8,128)(2,1)} %get-tuple-element.41) | data formatting | bytes 1310720
  157.0 0.0 copy-done
  157.0 0.8 copy.16
Async XLA Ops:
  153.0 4.0 %copy-start = (bf16[128,2560]{1,0:T(8,128)(2,1)S(1)}, bf16[128,2560]{1,0:T(8,128)(2,1)}, u32[]{:S(2)}) copy-start(bf16[128,2560]{1,0:T(8,128)(2,1)} %get-tuple-element.42) | copy-start | bytes 1966084

commit v3 on v2

--- a/solution.py
+++ b/solution.py
@@ -67,8 +67,8 @@
     pl.semaphore_wait(barrier, len(peers))
 
 
-DX = (0, 1, 3, 2)
 AHEAD = 6
+ORDER = (1, 3, 2, 0)
 BSTEP = 3
 
 
@@ -96,8 +96,8 @@
 
     def scatter_a(a, wave):
         dst = xa.at[x * 4 + y] if a == 4 else wide[a][1].at[rows(mine, BLK), :]
-        for dx in range(4):
-            dy = (dx + wave) % 4
+        dx = wave
+        for dy in (2, 1, 3, 0):
             tx, ty = (x + dx) % 4, (y + dy) % 4
             src = cut(a, ty * 4 + tx)
             if dx or dy:
@@ -117,7 +117,7 @@
             else:
                 pltpu.make_async_copy(cut(a, 16 + ty), dst, rb1.at[a]).start()
 
-    steps = [(a, wave) for wave in range(4) for a in (0, 2, 1, 3)]
+    steps = [(a, wave) for wave in (2, 1, 3, 0) for a in (0, 2, 1, 3)]
     for a in (0, 2, 1, 3):
         scatter_b(a)
     for step in steps[:AHEAD]:
@@ -134,9 +134,9 @@
         scatter_a(4, wave)
     scatter_b(4)
 
-    def part(a, ref, quad, wave, dx):
-        at = (quad * 4 + (x + 4 - dx) % 4) * 4 + (y + 8 - dx - wave) % 4
-        return ref.at[pl.ds(at, 1)] if a == 4 else ref.at[rows(at * BLK, BLK), :]
+    def part(a, ref, quad, dx):
+        at = quad * 4 + (x + 4 - dx) % 4
+        return ref.at[pl.ds(at * 4, 4)] if a == 4 else ref.at[rows(at * GROUP, GROUP), :]
 
     def whole(a, ref, count=4):
         return ref.at[pl.ds(0, count)] if a == 4 else ref.at[pl.ds(0, count * BLK), :]
@@ -147,16 +147,15 @@
     to_k = dev(x, k_pair(z), k, y)
     to_c = dev(x, z, 1 - k, y)
 
-    def forward_a(a, wave):
+    def forward_a(a, dx):
         ref = buf_a[a]
-        wait(whole(a, ref), ra1.at[a, wave])
-        for dx in range(4):
-            own, there = part(a, ref, 0, wave, dx), part(a, ref, 1, wave, dx)
-            if a in (2, 3):
-                send(own, there, s_zk.at[a - 2], r_zk.at[a - 2], to_k)
-            else:
-                send(own, there, s_zq.at[a], r_zq.at[a, wave], to_q)
-                send(own, part(a, ref, 2, wave, dx), s_c.at[a], r_c.at[a], to_c)
+        own, there = part(a, ref, 0, dx), part(a, ref, 1, dx)
+        wait(own, ra1.at[a, dx])
+        if a in (2, 3):
+            send(own, there, s_zk.at[a - 2], r_zk.at[a - 2], to_k)
+        else:
+            send(own, there, s_zq.at[a], r_zq.at[a, dx], to_q)
+            send(own, part(a, ref, 2, dx), s_c.at[a], r_c.at[a], to_c)
 
     def slab(a, ref, index, count=1):
         if a == 4:
@@ -213,12 +212,11 @@
             got = slab(a, ref, k * 4 + (z + 4 - dz) % 4)
             wait(got, r_bz.at[a, dz])
             send(got, got, s_bc.at[a], r_bc.at[a], to_c)
-    for wave in range(4):
+    for wave in (2, 1, 3, 0):
         for a in (0, 1, 4):
             ref = buf_a[a]
-            wait(whole(a, ref), r_zq.at[a, wave])
-            for dx in range(4):
-                send(part(a, ref, 1, wave, dx), part(a, ref, 3, wave, dx), s_c2.at[a], r_c2.at[a], to_c)
+            wait(part(a, ref, 1, wave), r_zq.at[a, wave])
+            send(part(a, ref, 1, wave), part(a, ref, 3, wave), s_c2.at[a], r_c2.at[a], to_c)
 
     def quad(a, ref, index):
         if a == 4:
@@ -317,19 +315,18 @@
 
     def turn(k_ref, n):
         def step(i, carry):
-            at = pl.ds(pl.multiple_of(i * BLK, BLK), BLK)
-            kt_ref[at, :] = k_ref[at, :].T
+            turned = k_ref[span(i), :].T
+            for b in range(4):
+                kt_ref[rows(i * GROUP + b * BLK, BLK), :] = turned[:, b * BLK:(b + 1) * BLK]
             return carry
 
-        lax.fori_loop(0, n, step, 0)
+        lax.fori_loop(0, n // 4, step, 0)
 
     def finish(dk_ref, dv_ref, n):
         def step(i, carry):
             at = span(i)
             dk_ref[at, :] = (acc_k[at, :] * SCALE).astype(BF)
             dv_ref[at, :] = acc_v[at, :].astype(BF)
-            acc_k[at, :] = jnp.zeros((GROUP, BLK), F32)
-            acc_v[at, :] = jnp.zeros((GROUP, BLK), F32)
             return carry
 
         lax.fori_loop(0, n, step, 0)
@@ -410,11 +407,8 @@
     late = pl.ds(4 * GROUP, 12 * GROUP)
     store(dqa.at[late, :], dqa_out.at[late, :])
 
-    def diag_a(q, carry):
+    for q in range(4):
         diag(qa, ga, xa, ka, va, dqa, q, index_a(q), q)
-        return carry
-
-    lax.fori_loop(0, 4, diag_a, 0)
     early = pl.ds(0, 4 * GROUP)
     store(dqa.at[early, :], dqa_out.at[early, :])
     finish(dka, dva, 8)
@@ -423,6 +417,8 @@
     for load in loads[5:]:
         load.wait()
 
+    acc_k[0:16 * BLK, :] = jnp.zeros((16 * BLK, BLK), F32)
+    acc_v[0:16 * BLK, :] = jnp.zeros((16 * BLK, BLK), F32)
     turn(kb, 16)
     main(qb, gb, xb, kb, vb, dqb, 8, lambda q: x * 8 + (q % 4) * 2 + q // 4, [(0, lambda i: i * 8 + z * 2 + k)])
     diag(qb, gb, xb, kb, vb, dqb, k * 4 + z, x * 8 + z * 2 + k, x)
@@ -489,38 +485,11 @@
     def slab(ref, index):
         return ref.at[rows(index * GROUP, GROUP), :]
 
-    for dx in DX:
-        send(chunk(dqa, 3, dx), chunk(got_c, 1, dx), s_c, r_c.at[1, dx], to_c)
-    send(dqb.at[rows((1 - k) * 4 * GROUP, 4 * GROUP), :], bgot_c, s_bc, r_bc, to_c)
-    for dx in DX:
-        for n, src in enumerate((dka, dva)):
-            send(chunk(src, 1, dx), chunk(got_zk.at[n], 0, dx), s_zk, r_zk.at[n, dx], to_k)
-    for dx in DX:
-        send(chunk(dqa, 2, dx), chunk(got_c, 0, dx), s_c, r_c.at[0, dx], to_c)
-    for dx in (1, 3, 2):
-        for n, src in enumerate((dkb, dvb)):
-            send(slab(src, (x + dx) % 4), slab(bgot_x.at[n], dx - 1), s_bx, r_bx.at[n, dx - 1], dev((x + dx) % 4, z, k, y))
-
     def add(*refs):
         total = refs[0][...].astype(F32)
         for ref in refs[1:]:
             total = total + ref[...].astype(F32)
         return total.astype(BF)
-
-    for load in loads:
-        load.wait()
-
-    for dx in DX:
-        wait(chunk(got_c, 1, dx), r_c.at[1, dx])
-        part = chunk(put_zq, 0, dx)
-        part[...] = add(chunk(own_q, 1, dx), chunk(got_c, 1, dx))
-        send(part, chunk(got_zq, 0, dx), s_zq, r_zq.at[dx], to_q)
-    wait(bgot_c, r_bc)
-    for dz in (1, 3, 2):
-        zt = (z + dz) % 4
-        part = slab(bput_q, zt)
-        part[...] = add(slab(own_bq, zt), slab(bgot_c, zt))
-        send(part, slab(bgot_z, dz - 1), s_bz, r_bz.at[dz - 1], dev(x, zt, k, y))
 
     def give(n, src, base, tx, head_of, dx):
         for dy in range(4):
@@ -532,29 +501,81 @@
             else:
                 pltpu.make_async_copy(block, dst, r_out.at[n]).start()
 
-    for dx in (1, 3, 2, 0):
+    def keys_out(dx):
+        for n, src in enumerate((dka, dva)):
+            send(chunk(src, 1, dx), chunk(got_zk.at[n], 0, dx), s_zk, r_zk.at[n, dx], to_k)
+
+    def far_keys_out(dx):
+        for n, src in enumerate((dkb, dvb)):
+            to = dev((x + dx) % 4, z, k, y)
+            send(slab(src, (x + dx) % 4), slab(bgot_x.at[n], dx - 1), s_bx, r_bx.at[n, dx - 1], to)
+
+    def queries_on(dx):
+        wait(chunk(got_c, 1, dx), r_c.at[1, dx])
+        part = chunk(put_zq, 0, dx)
+        part[...] = add(chunk(own_q, 1, dx), chunk(got_c, 1, dx))
+        send(part, chunk(got_zq, 0, dx), s_zq, r_zq.at[dx], to_q)
+
+    def far_queries_on(dz):
+        zt = (z + dz) % 4
+        part = slab(bput_q, zt)
+        part[...] = add(slab(own_bq, zt), slab(bgot_c, zt))
+        send(part, slab(bgot_z, dz - 1), s_bz, r_bz.at[dz - 1], dev(x, zt, k, y))
+
+    def keys_home(dx):
         tx = (x + dx) % 4
         for n, own in ((1, own_k), (2, own_v)):
             wait(chunk(got_zk.at[n - 1], 0, dx), r_zk.at[n - 1, dx])
             out = chunk(fin.at[n], 0, dx)
             out[...] = add(chunk(own, 0, dx), chunk(got_zk.at[n - 1], 0, dx))
             give(n, fin.at[n], tx * GROUP, tx, y * 4 + x, dx)
-    for dx in (1, 3, 2, 0):
+
+    def queries_home(dx):
         tx = (x + dx) % 4
         wait(chunk(got_c, 0, dx), r_c.at[0, dx])
         wait(chunk(got_zq, 0, dx), r_zq.at[dx])
         out = chunk(fin.at[0], 0, dx)
         out[...] = add(chunk(own_q, 0, dx), chunk(got_c, 0, dx), chunk(got_zq, 0, dx))
         give(0, fin.at[0], tx * GROUP, tx, y * 4 + x, dx)
-    for n, own in ((1, own_bk), (2, own_bv)):
+
+    def far_keys_home():
+        for n, own in ((1, own_bk), (2, own_bv)):
+            for i in range(3):
+                wait(slab(bgot_x.at[n - 1], i), r_bx.at[n - 1, i])
+            bfin[n] = add(own, *[slab(bgot_x.at[n - 1], i) for i in range(3)])
+            give(n, bfin.at[n], 0, x, 16 + y, 0)
+
+    def far_queries_home():
         for i in range(3):
-            wait(slab(bgot_x.at[n - 1], i), r_bx.at[n - 1, i])
-        bfin[n] = add(own, *[slab(bgot_x.at[n - 1], i) for i in range(3)])
-        give(n, bfin.at[n], 0, x, 16 + y, 0)
-    for i in range(3):
-        wait(slab(bgot_z, i), r_bz.at[i])
-    bfin[0] = add(slab(own_bq, z), slab(bgot_c, z), *[slab(bgot_z, i) for i in range(3)])
-    give(0, bfin.at[0], 0, x, 16 + y, 0)
+            wait(slab(bgot_z, i), r_bz.at[i])
+        bfin[0] = add(slab(own_bq, z), slab(bgot_c, z), *[slab(bgot_z, i) for i in range(3)])
+        give(0, bfin.at[0], 0, x, 16 + y, 0)
+
+    first, second, third, last = ORDER
+    for dx in ORDER:
+        send(chunk(dqa, 3, dx), chunk(got_c, 1, dx), s_c, r_c.at[1, dx], to_c)
+    send(dqb.at[rows((1 - k) * 4 * GROUP, 4 * GROUP), :], bgot_c, s_bc, r_bc, to_c)
+    keys_out(first)
+    far_keys_out(1)
+    far_keys_out(3)
+    for load in loads:
+        load.wait()
+    for dx in ORDER:
+        send(chunk(dqa, 2, dx), chunk(got_c, 0, dx), s_c, r_c.at[0, dx], to_c)
+    for dx in ORDER:
+        queries_on(dx)
+    far_keys_out(2)
+    for dx in ORDER[1:]:
+        keys_out(dx)
+    wait(bgot_c, r_bc)
+    for dz in (1, 3, 2):
+        far_queries_on(dz)
+    for dx in ORDER:
+        queries_home(dx)
+        keys_home(dx)
+        if dx == 1:
+            far_keys_home()
+    far_queries_home()
 
     for n in range(3):
         wait(outs[n], r_out.at[n])

time: 159 us -> 144 us (0.906)
  Pallas kernels: 152 us -> 136 us
    pallas_call x1, Pallas kernels: 51.4 us -> 41.3 us  [body(): pl.pallas_call(return_kernel, out_shape=(flat, flat, flat), in_specs=[any...]
    pallas_call x1, Pallas kernels: 59.1 us -> 55.2 us  [body(): pl.pallas_call(gather_kernel, out_shape=(wide(64), wide(64), aux(64), wid...]
    pallas_call x1, Pallas kernels: 41.8 us -> 39.6 us  [compute_call(): pl.pallas_call(compute_kernel, out_shape=(wide(64), wide(32), wide(32), w...]
where the time goes in v3:
time: 144 us; the launch traced here: 142 us
  Pallas kernels  136 us (94%)
  local copies, waits for them, and re-layouts  4.84 us (3%)
    pallas_call x1, Pallas kernels, body(): pl.pallas_call(gather_kernel, out_shape=(wide(64), wide(64), aux(64), wid...  55.2 us
    pallas_call x1, Pallas kernels, body(): pl.pallas_call(return_kernel, out_shape=(flat, flat, flat), in_specs=[any...  41.3 us
    pallas_call x1, Pallas kernels, compute_call(): pl.pallas_call(compute_kernel, out_shape=(wide(64), wide(32), wide(32), w...  39.6 us
    unnamed x5, local copies, waits for them, and re-layouts  4.84 us

profile of v3, /device:TPU:32, one launch (start us, length us, event | category | flops | bytes accessed | tf_op | source)
XLA Modules:
  0.0 141.6 jit_solution(389147563073947446)
XLA Ops:
  0.6 55.2 %gather_blocks.1 = (bf16[8192,128]{1,0:T(8,128)(2,1)}, bf16[8192,128]{1,0:T(8,128)(2,1)}, f32[64,8,128]{2,1,0:T(8,128)}, bf16[4096,128]{1,0:T(8,128)(2,1)}, bf16...) custom-call(bf16[128,2560]{1,0:T(8,128)(2,1)} %q_in.1, ...), custom_call_target="tpu_custom_call" | custom-call | tf_op jit(solution)/shard_map/gather_blocks/pallas_call | solution.py:601
  55.8 39.6 %block_grads.1 = (bf16[8192,128]{1,0:T(8,128)(2,1)}, bf16[4096,128]{1,0:T(8,128)(2,1)}, bf16[4096,128]{1,0:T(8,128)(2,1)}, bf16[4096,128]{1,0:T(8,128)(2,1)}, bf...) custom-call(s32[128,128]{1,0:T(8,128)} %get-tuple-element.20.table, bf16[8192,128]{1,0:T(8,128)(2,1)} %get-tuple-element.21.qa_in, ...), custom_call_target="tpu_custom_call" | custom-call | tf_op jit(solution)/shard_map/block_grads/pallas_call | solution.py:438
  95.4 41.3 %return_grads.1 = (bf16[128,2560]{1,0:T(8,128)(2,1)}, bf16[128,2560]{1,0:T(8,128)(2,1)}, bf16[128,2560]{1,0:T(8,128)(2,1)}) custom-call(bf16[8192,128]{1,0:T(8,128)(2,1)} %get-tuple-element.31.dqa, bf16[4096,128]{1,0:T(8,128)(2,1)} %get-tuple-element.32.dka, bf16[4096,128]{1,0:T(8,128)(2,1)} %get-tuple-element.33.dva, ...), custom_call_target="tpu_custom_call" | custom-call | tf_op jit(solution)/shard_map/return_grads/pallas_call | solution.py:628
  136.7 0.0 copy-start
  136.7 2.0 %copy.14 = bf16[128,2560]{1,0:T(8,128)(2,1)} copy(bf16[128,2560]{1,0:T(8,128)(2,1)} %get-tuple-element.40) | data formatting | bytes 1310720
  138.8 2.0 %copy.15 = bf16[128,2560]{1,0:T(8,128)(2,1)} copy(bf16[128,2560]{1,0:T(8,128)(2,1)} %get-tuple-element.41) | data formatting | bytes 1310720
  140.7 0.0 copy-done
  140.7 0.8 copy.16
Async XLA Ops:
  136.7 4.0 %copy-start = (bf16[128,2560]{1,0:T(8,128)(2,1)S(1)}, bf16[128,2560]{1,0:T(8,128)(2,1)}, u32[]{:S(2)}) copy-start(bf16[128,2560]{1,0:T(8,128)(2,1)} %get-tuple-element.42) | copy-start | bytes 1966084

commit v4 on v3

--- a/solution.py
+++ b/solution.py
@@ -70,12 +70,13 @@
 AHEAD = 6
 ORDER = (1, 3, 2, 0)
 BSTEP = 3
+SPLIT = 4
 
 
 def gather_kernel(
     q_in, k_in, v_in, g_in, o_in, norm_in, pat_in, order_in,
     qa, ga, xa, ka, va, qb, gb, xb, kb, vb, table,
-    g_v, o_v, aux, pat_v,
+    g_v, o_v, aux, pat_v, own_v, own_sem,
     load_sem, sa1, ra1, sb1, rb1, s_zq, r_zq, s_c, r_c, s_c2, r_c2, s_zk, r_zk,
     s_bz, r_bz, s_bc, r_bc, s_bx, r_bx,
 ):
@@ -84,6 +85,13 @@
     load_o = pltpu.make_async_copy(o_in, o_v, load_sem.at[1])
     load_g.start()
     load_o.start()
+    own_loads = [
+        pltpu.make_async_copy(ref.at[:, cols(head)], own_v.at[i * 4 + a], own_sem.at[i * 4 + a])
+        for i, head in enumerate((y * 4 + x, 16 + y))
+        for a, ref in enumerate((q_in, g_in, k_in, v_in))
+    ]
+    for load in own_loads:
+        load.start()
     greet()
     mine = (x * 4 + y) * BLK
 
@@ -103,6 +111,9 @@
             if dx or dy:
                 send(src, dst, sa1.at[a], ra1.at[a, wave], dev(tx, z, k, ty))
             else:
+                if a < 4:
+                    own_loads[a].wait()
+                    src = own_v.at[a]
                 pltpu.make_async_copy(src, dst, ra1.at[a, wave]).start()
 
     def scatter_b(a):
@@ -115,7 +126,10 @@
             if dy:
                 send(cut(a, 16 + ty), dst, sb1.at[a], rb1.at[a], dev(x, z, k, ty))
             else:
-                pltpu.make_async_copy(cut(a, 16 + ty), dst, rb1.at[a]).start()
+                if a < 4:
+                    own_loads[4 + a].wait()
+                src = own_v.at[4 + a] if a < 4 else cut(a, 16 + ty)
+                pltpu.make_async_copy(src, dst, rb1.at[a]).start()
 
     steps = [(a, wave) for wave in (2, 1, 3, 0) for a in (0, 2, 1, 3)]
     for a in (0, 2, 1, 3):
@@ -261,7 +275,7 @@
         (kb_in, kb), (vb_in, vb), (qb_in, qb), (gb_in, gb), (xb_in, xb),
     ]
     loads = [pltpu.make_async_copy(src, dst, in_sem.at[i]) for i, (src, dst) in enumerate(pairs_in)]
-    for load in loads:
+    for load in loads[:5]:
         load.start()
     stores = []
 
@@ -309,8 +323,9 @@
         dv = jnp.dot(p[...], g_ref[span(q), :], preferred_element_type=F32)
         dq = jnp.dot(blocks(kt_ref, places, 1), e[...], preferred_element_type=F32)
         for i, at in enumerate(places):
-            acc_k[pl.ds(at, BLK), :] += dk[i * BLK:(i + 1) * BLK]
-            acc_v[pl.ds(at, BLK), :] += dv[i * BLK:(i + 1) * BLK]
+            inner = pl.ds(pl.multiple_of(at - i * GROUP, BLK), BLK)
+            acc_k[i][inner, :] += dk[i * BLK:(i + 1) * BLK]
+            acc_v[i][inner, :] += dv[i * BLK:(i + 1) * BLK]
         dq_ref[span(q), :] = (dq * SCALE).T.astype(BF)
 
     def turn(k_ref, n):
@@ -323,13 +338,10 @@
         lax.fori_loop(0, n // 4, step, 0)
 
     def finish(dk_ref, dv_ref, n):
-        def step(i, carry):
-            at = span(i)
-            dk_ref[at, :] = (acc_k[at, :] * SCALE).astype(BF)
-            dv_ref[at, :] = acc_v[at, :].astype(BF)
-            return carry
-
-        lax.fori_loop(0, n, step, 0)
+        for i in range(n):
+            at = pl.ds(i * GROUP, GROUP)
+            dk_ref[at, :] = (acc_k[i][...] * SCALE).astype(BF)
+            dv_ref[at, :] = acc_v[i][...].astype(BF)
 
     def main(q_ref, g_ref, x_ref, k_ref, v_ref, dq_ref, count, c_of, groups):
         n = len(groups) * GROUP
@@ -384,13 +396,25 @@
             scores.append(score_e)
         prob = jnp.concatenate(probs, axis=0)
         score = jnp.concatenate(scores, axis=0)
-        acc_k[here, :] += jnp.dot(score, query, preferred_element_type=F32)
-        acc_v[here, :] += jnp.dot(prob, grad, preferred_element_type=F32)
+        dk = jnp.dot(score, query, preferred_element_type=F32)
+        dv = jnp.dot(prob, grad, preferred_element_type=F32)
+        if isinstance(own, int):
+            acc_k[own][...] += dk
+            acc_v[own][...] += dv
+        else:
+            for i in range(4):
+                @pl.when(own == i)
+                def _(i=i):
+                    acc_k[i][...] += dk
+                    acc_v[i][...] += dv
         dq = jnp.dot(blocks(kt_ref, places, 1), score, preferred_element_type=F32)
         dq_ref[span(q), :] = (dq_ref[span(q), :].astype(F32) + (dq * SCALE).T).astype(BF)
 
-    acc_k[...] = jnp.zeros_like(acc_k)
-    acc_v[...] = jnp.zeros_like(acc_v)
+    def clear(n):
+        for ref in (*acc_k[:n], *acc_v[:n]):
+            ref[...] = jnp.zeros((GROUP, BLK), F32)
+
+    clear(8)
 
     def index_a(q):
         quad, xq = q // 4, q % 4
@@ -402,6 +426,8 @@
     turn(ka, 32)
     for load in loads[1:5]:
         load.wait()
+    for load in loads[5:]:
+        load.start()
     main(qa, ga, xa, ka, va, dqa, 16, index_a, [(0, lambda i: i * 8 + z * 2 + k), (4, lambda i: i * 8 + zk * 2 + k)])
 
     late = pl.ds(4 * GROUP, 12 * GROUP)
@@ -417,8 +443,7 @@
     for load in loads[5:]:
         load.wait()
 
-    acc_k[0:16 * BLK, :] = jnp.zeros((16 * BLK, BLK), F32)
-    acc_v[0:16 * BLK, :] = jnp.zeros((16 * BLK, BLK), F32)
+    clear(4)
     turn(kb, 16)
     main(qb, gb, xb, kb, vb, dqb, 8, lambda q: x * 8 + (q % 4) * 2 + q // 4, [(0, lambda i: i * 8 + z * 2 + k)])
     diag(qb, gb, xb, kb, vb, dqb, k * 4 + z, x * 8 + z * 2 + k, x)
@@ -444,7 +469,7 @@
             hold(64), hold(64), aux(64), hold(32), hold(32), hold(32), hold(32), aux(32), hold(16), hold(16),
             hold(64), hold(32), hold(32), hold(32), hold(16), hold(16),
             pltpu.SemaphoreType.DMA((10,)), pltpu.SemaphoreType.DMA((7,)),
-            VMEM((32 * BLK, BLK), F32), VMEM((32 * BLK, BLK), F32), hold(32),
+            [VMEM((GROUP, BLK), F32)] * 8, [VMEM((GROUP, BLK), F32)] * 8, hold(32),
             VMEM((2, 8 * BLK, GROUP), F32), VMEM((2, 8 * BLK, GROUP), F32),
             VMEM((2, 8 * BLK, GROUP), BF), VMEM((2, 8 * BLK, GROUP), BF),
         ],
@@ -588,6 +613,25 @@
     wait(dqa.at[pl.ds(0, 6 * GROUP), :], s_bx)
 
 
+def hand_out_kernel(dq, dk, dv, dq_out, dk_out, dv_out, held, sems):
+    part = dq.shape[0] // SPLIT
+    pieces = [(n, i) for i in range(SPLIT) for n in range(3)]
+    src, dst = (dq, dk, dv), (dq_out, dk_out, dv_out)
+
+    def cut(ref, i):
+        return ref.at[pl.ds(i * part, part), :]
+
+    loads = [pltpu.make_async_copy(cut(src[n], i), cut(held.at[n], i), sems.at[0, n, i]) for n, i in pieces]
+    stores = [pltpu.make_async_copy(cut(held.at[n], i), cut(dst[n], i), sems.at[1, n, i]) for n, i in pieces]
+    for load in loads:
+        load.start()
+    for load, store in zip(loads, stores):
+        load.wait()
+        store.start()
+    for store in stores:
+        store.wait()
+
+
 def body(queries, key_rows, value_rows, forward_out, out_grad, log_norm, block_order, pattern):
     wide = lambda n: jax.ShapeDtypeStruct((n * BLK, BLK), BF)
     aux = lambda n: jax.ShapeDtypeStruct((n, 8, BLK), F32)
@@ -609,7 +653,7 @@
         out_specs=(any_,) * 10 + (vmem,),
         scratch_shapes=[
             VMEM((tokens, width), BF), VMEM((tokens, width), BF), VMEM((HEADS, 8, BLK), F32),
-            VMEM((BLK, BLK), F32),
+            VMEM((BLK, BLK), F32), VMEM((8, BLK, BLK), BF), sem(8),
             sem(2), sem(5), sem(5, 4), sem(5), sem(5), sem(5), sem(5, 4), sem(5), sem(5), sem(5), sem(5), sem(2), sem(2),
             sem(5), sem(5, 4), sem(5), sem(5), sem(2), sem(2),
         ],
@@ -625,7 +669,7 @@
 
     grads = compute_call(table, *gathered[:10])
     flat = jax.ShapeDtypeStruct((tokens, width), BF)
-    return pl.pallas_call(
+    landed = pl.pallas_call(
         return_kernel,
         out_shape=(flat, flat, flat),
         in_specs=[any_] * 6,
@@ -643,6 +687,15 @@
         ),
         name="return_grads",
     )(*grads)
+    return pl.pallas_call(
+        hand_out_kernel,
+        out_shape=(flat, flat, flat),
+        in_specs=[any_] * 3,
+        out_specs=(any_,) * 3,
+        scratch_shapes=[VMEM((3, tokens, width), BF), sem(2, 3, SPLIT)],
+        compiler_params=pltpu.CompilerParams(vmem_limit_bytes=VMEM_LIMIT),
+        name="hand_out",
+    )(*landed)
 
 
 def solution(mesh):

time: 144 us -> 141 us (0.979)
  local copies, waits for them, and re-layouts: 4.84 us -> 0 us
  Pallas kernels: 136 us -> 139 us
    unnamed x5 -> x0, local copies, waits for them, and re-layouts: 4.84 us -> none
    pallas_call x0 -> x1, Pallas kernels: none -> 2.49 us  [body(): pl.pallas_call(hand_out_kernel, out_shape=(flat, flat, flat), in_specs=[a...]
where the time goes in v4:
time: 141 us; the launch traced here: 140 us
  Pallas kernels  139 us (99%)
    pallas_call x1, Pallas kernels, body(): pl.pallas_call(gather_kernel, out_shape=(wide(64), wide(64), aux(64), wid...  55.3 us
    pallas_call x1, Pallas kernels, body(): pl.pallas_call(return_kernel, out_shape=(flat, flat, flat), in_specs=[any...  41.3 us
    pallas_call x1, Pallas kernels, compute_call(): pl.pallas_call(compute_kernel, out_shape=(wide(64), wide(32), wide(32), w...  39.5 us

profile of v4, /device:TPU:32, one launch (start us, length us, event | category | flops | bytes accessed | tf_op | source)
XLA Modules:
  0.0 139.5 jit_solution(10963063986674579935)
XLA Ops:
  0.6 55.3 %gather_blocks.1 = (bf16[8192,128]{1,0:T(8,128)(2,1)}, bf16[8192,128]{1,0:T(8,128)(2,1)}, f32[64,8,128]{2,1,0:T(8,128)}, bf16[4096,128]{1,0:T(8,128)(2,1)}, bf16...) custom-call(bf16[128,2560]{1,0:T(8,128)(2,1)} %q_in.1, ...), custom_call_target="tpu_custom_call" | custom-call | tf_op jit(solution)/shard_map/gather_blocks/pallas_call | solution.py:645
  56.0 39.5 %block_grads.1 = (bf16[8192,128]{1,0:T(8,128)(2,1)}, bf16[4096,128]{1,0:T(8,128)(2,1)}, bf16[4096,128]{1,0:T(8,128)(2,1)}, bf16[4096,128]{1,0:T(8,128)(2,1)}, bf...) custom-call(s32[128,128]{1,0:T(8,128)} %get-tuple-element.23.table, bf16[8192,128]{1,0:T(8,128)(2,1)} %get-tuple-element.24.qa_in, ...), custom_call_target="tpu_custom_call" | custom-call | tf_op jit(solution)/shard_map/block_grads/pallas_call | solution.py:463
  95.5 41.3 %return_grads.1 = (bf16[128,2560]{1,0:T(8,128)(2,1)}, bf16[128,2560]{1,0:T(8,128)(2,1)}, bf16[128,2560]{1,0:T(8,128)(2,1)}) custom-call(bf16[8192,128]{1,0:T(8,128)(2,1)} %get-tuple-element.34.dqa, bf16[4096,128]{1,0:T(8,128)(2,1)} %get-tuple-element.35.dka, bf16[4096,128]{1,0:T(8,128)(2,1)} %get-tuple-element.36.dva, ...), custom_call_target="tpu_custom_call" | custom-call | tf_op jit(solution)/shard_map/return_grads/pallas_call | solution.py:672
  136.9 2.5 %hand_out.1 = (bf16[128,2560]{1,0:T(8,128)(2,1)}, bf16[128,2560]{1,0:T(8,128)(2,1)}, bf16[128,2560]{1,0:T(8,128)(2,1)}) custom-call(bf16[128,2560]{1,0:T(8,128)(2,1)} %get-tuple-element.40.dq, bf16[128,2560]{1,0:T(8,128)(2,1)} %get-tuple-element.41.dk, bf16[128,2560]{1,0:T(8,128)(2,1)} %get-tuple-element.42.dv), custom_call_target="tpu_custom_call" | custom-call | tf_op jit(solution)/shard_map/hand_out/pallas_call | solution.py:690

commit v5 on v4

--- a/solution.py
+++ b/solution.py
@@ -70,6 +70,7 @@
 AHEAD = 6
 ORDER = (1, 3, 2, 0)
 BSTEP = 3
+RELAY = 11
 SPLIT = 4
 
 
@@ -181,19 +182,43 @@
             ref = buf_b[a]
             own = slab(a, ref, slot)
             wait(own, rb1.at[a])
-            for dz in (1, 3, 2):
+            for dz in (1, 3):
                 send(own, own, s_bz.at[a], r_bz.at[a, dz], dev(x, (z + dz) % 4, k, y))
             send(own, own, s_bc.at[a], r_bc.at[a], to_c)
         for a in (2, 3):
             ref = buf_b[a]
             own = slab(a, ref, x)
             wait(own, rb1.at[a])
-            for dx in (1, 3, 2):
-                send(own, own, s_bx.at[a - 2], r_bx.at[a - 2], dev((x + dx) % 4, z, k, y))
+            for dx in (1, 3):
+                send(own, own, s_bx.at[a - 2], r_bx.at[a - 2, dx], dev((x + dx) % 4, z, k, y))
+
+    def half(a, ref, index, h):
+        if a == 4:
+            return ref.at[pl.ds(index * 4 + h * 2, 2)]
+        return ref.at[rows(index * GROUP + h * 2 * BLK, 2 * BLK), :]
+
+    def relay_b():
+        for a in (0, 2, 1, 3, 4):
+            ref = buf_b[a]
+            for h, d in ((0, 1), (1, 3)):
+                if a in (2, 3):
+                    index = (x + 4 - d) % 4
+                    wait(slab(a, ref, index), r_bx.at[a - 2, d])
+                    piece = half(a, ref, index, h)
+                    send(piece, piece, s_bx.at[a - 2], r_bx.at[a - 2, 2], dev((x + d) % 4, z, k, y))
+                else:
+                    index = k * 4 + (z + 4 - d) % 4
+                    got = slab(a, ref, index)
+                    wait(got, r_bz.at[a, d])
+                    piece = half(a, ref, index, h)
+                    send(piece, piece, s_bz.at[a], r_bz.at[a, 2], dev(x, (z + d) % 4, k, y))
+                    send(got, got, s_bc.at[a], r_bc.at[a], to_c)
 
     for n, step in enumerate(steps):
         if n == BSTEP:
             forward_b()
+        if n == RELAY:
+            relay_b()
         forward_a(*step)
         if n + AHEAD < 16:
             scatter_a(*steps[n + AHEAD])
@@ -220,12 +245,11 @@
         + jnp.dot(jnp.where(local, adj, 0.0).astype(BF), own_cols.astype(BF), preferred_element_type=F32)
     ).astype(jnp.int32)
 
-    for dz in (1, 3, 2):
-        for a in (0, 1, 4):
-            ref = buf_b[a]
-            got = slab(a, ref, k * 4 + (z + 4 - dz) % 4)
-            wait(got, r_bz.at[a, dz])
-            send(got, got, s_bc.at[a], r_bc.at[a], to_c)
+    for a in (0, 1, 4):
+        ref = buf_b[a]
+        got = slab(a, ref, k * 4 + (z + 2) % 4)
+        wait(got, r_bz.at[a, 2])
+        send(got, got, s_bc.at[a], r_bc.at[a], to_c)
     for wave in (2, 1, 3, 0):
         for a in (0, 1, 4):
             ref = buf_a[a]
@@ -240,7 +264,7 @@
     for a in (2, 3):
         wait(quad(a, buf_a[a], 1), r_zk.at[a - 2])
         wait(quad(a, buf_a[a], 0), s_zk.at[a - 2])
-        wait(slab(a, buf_b[a], 0, 3), r_bx.at[a - 2])
+        wait(slab(a, buf_b[a], 0), r_bx.at[a - 2, 2])
         wait(slab(a, buf_b[a], 0, 3), s_bx.at[a - 2])
     for a in (0, 1, 4):
         wait(quad(a, buf_a[a], 2), r_c.at[a])
@@ -655,7 +679,7 @@
             VMEM((tokens, width), BF), VMEM((tokens, width), BF), VMEM((HEADS, 8, BLK), F32),
             VMEM((BLK, BLK), F32), VMEM((8, BLK, BLK), BF), sem(8),
             sem(2), sem(5), sem(5, 4), sem(5), sem(5), sem(5), sem(5, 4), sem(5), sem(5), sem(5), sem(5), sem(2), sem(2),
-            sem(5), sem(5, 4), sem(5), sem(5), sem(2), sem(2),
+            sem(5), sem(5, 4), sem(5), sem(5), sem(2), sem(2, 4),
         ],
         compiler_params=pltpu.CompilerParams(
             collective_id=0, has_side_effects=True, vmem_limit_bytes=VMEM_LIMIT

time: 141 us -> 138 us (0.979)
  Pallas kernels: 139 us -> 135 us
    pallas_call x1, Pallas kernels: 55.3 us -> 53.7 us  [body(): pl.pallas_call(gather_kernel, out_shape=(wide(64), wide(64), aux(64), wid...]
    pallas_call x1, Pallas kernels: 41.3 us -> 39.7 us  [body(): pl.pallas_call(return_kernel, out_shape=(flat, flat, flat), in_specs=[any...]
where the time goes in v5:
time: 138 us; the launch traced here: 136 us
  Pallas kernels  135 us (98%)
    pallas_call x1, Pallas kernels, body(): pl.pallas_call(gather_kernel, out_shape=(wide(64), wide(64), aux(64), wid...  53.7 us
    pallas_call x1, Pallas kernels, body(): pl.pallas_call(return_kernel, out_shape=(flat, flat, flat), in_specs=[any...  39.7 us
    pallas_call x1, Pallas kernels, compute_call(): pl.pallas_call(compute_kernel, out_shape=(wide(64), wide(32), wide(32), w...  39.5 us

profile of v5, /device:TPU:32, one launch (start us, length us, event | category | flops | bytes accessed | tf_op | source)
XLA Modules:
  0.0 136.3 jit_solution(8570224793527096537)
XLA Ops:
  0.6 53.7 %gather_blocks.1 = (bf16[8192,128]{1,0:T(8,128)(2,1)}, bf16[8192,128]{1,0:T(8,128)(2,1)}, f32[64,8,128]{2,1,0:T(8,128)}, bf16[4096,128]{1,0:T(8,128)(2,1)}, bf16...) custom-call(bf16[128,2560]{1,0:T(8,128)(2,1)} %q_in.1, ...), custom_call_target="tpu_custom_call" | custom-call | tf_op jit(solution)/shard_map/gather_blocks/pallas_call | solution.py:669
  54.4 39.5 %block_grads.1 = (bf16[8192,128]{1,0:T(8,128)(2,1)}, bf16[4096,128]{1,0:T(8,128)(2,1)}, bf16[4096,128]{1,0:T(8,128)(2,1)}, bf16[4096,128]{1,0:T(8,128)(2,1)}, bf...) custom-call(s32[128,128]{1,0:T(8,128)} %get-tuple-element.23.table, bf16[8192,128]{1,0:T(8,128)(2,1)} %get-tuple-element.24.qa_in, ...), custom_call_target="tpu_custom_call" | custom-call | tf_op jit(solution)/shard_map/block_grads/pallas_call | solution.py:487
  93.9 39.7 %return_grads.1 = (bf16[128,2560]{1,0:T(8,128)(2,1)}, bf16[128,2560]{1,0:T(8,128)(2,1)}, bf16[128,2560]{1,0:T(8,128)(2,1)}) custom-call(bf16[8192,128]{1,0:T(8,128)(2,1)} %get-tuple-element.34.dqa, bf16[4096,128]{1,0:T(8,128)(2,1)} %get-tuple-element.35.dka, bf16[4096,128]{1,0:T(8,128)(2,1)} %get-tuple-element.36.dva, ...), custom_call_target="tpu_custom_call" | custom-call | tf_op jit(solution)/shard_map/return_grads/pallas_call | solution.py:696
  133.6 2.5 %hand_out.1 = (bf16[128,2560]{1,0:T(8,128)(2,1)}, bf16[128,2560]{1,0:T(8,128)(2,1)}, bf16[128,2560]{1,0:T(8,128)(2,1)}) custom-call(bf16[128,2560]{1,0:T(8,128)(2,1)} %get-tuple-element.40.dq, bf16[128,2560]{1,0:T(8,128)(2,1)} %get-tuple-element.41.dk, bf16[128,2560]{1,0:T(8,128)(2,1)} %get-tuple-element.42.dv), custom_call_target="tpu_custom_call" | custom-call | tf_op jit(solution)/shard_map/hand_out/pallas_call | solution.py:714
